TPU v7x, 512 devices: a whole 4x8x8 slice. The times are simulated.
512 devices in a mesh: resp: 64 (over z, y_hi, x), head: 8 (over y_lo, core).
Axes of the slice: x: 4, y: 8 (y_hi: 2, y_lo: 4; y = y_hi * 4 + y_lo), z: 8, core: 2. Of those that a mesh axis runs over, the one named last changes fastest.
Arguments:
- ssm_input: bfloat16 [32768, 8192], P('resp', 'head'), may hold values from -6 to 6
- b_proj: bfloat16 [32768, 1024], P('resp', 'head'), may hold values from -0.5 to 0.5
- c_proj: bfloat16 [32768, 1024], P('resp', 'head'), may hold values from -6 to 6
- step_size: float32 [32768, 128], P('resp', 'head'), may hold values from 0.02 to 0.2
- a_log: float32 [128], P('head'), may hold values from -3 to 1.5
- d_skip: float32 [128], P('head'), may hold values from 0.5 to 1.5
- out_weight: bfloat16 [8192, 2048], P(('head', 'resp')), may hold values from -0.0625 to 0.0625
- prompt_state: bfloat16 [64, 128, 64, 128], P('resp', 'head'), may hold values from -0.59765625 to 0.59765625
- prompt_of: int32 [512], P('resp'), may hold values from 0 to 63, as said below
- out_grad: bfloat16 [32768, 2048], P(('resp', 'head')), may hold values from -6 to 6
Outputs:
- layer_out: bfloat16 [32768, 2048], P(('resp', 'head'))
- grad_input: bfloat16 [32768, 8192], P('resp', 'head')
- grad_state: float32 [64, 128, 64, 128], P('resp', 'head')
Inputs may be any that keep to these rules, and one draw needn't show every extreme that they name: `prompt_of`: for every g, responses 8 * 8 * g to 8 * 8 * (g + 1) - 1 name only prompts 8 * g to 8 * (g + 1) - 1, and every prompt is named by exactly 8 responses.
All inputs are finite; a program needn't handle non-finite values.
Results may differ from a plain program's by a relative error of at most 0.0051.
Values may be sent and summed in bfloat16 or wider, within the bound.
A program may use at most 64 MiB of HBM per device.

v0:
```python
import jax
import jax.numpy as jnp
from jax import lax
from jax.sharding import PartitionSpec as P

NS = 128
FAN = 8


def partner(shard, axis, apart):
    return lax.ppermute(shard, axis, [(i, i ^ 1 << apart) for i in range(lax.axis_size(axis))])


def swap_states(value, bit_number):
    return partner(value, "resp", bit_number)


def swap_grads(value, bit_number):
    return partner(value, "resp", bit_number)


def per_device(
    ssm_input,
    b_proj,
    c_proj,
    step_size,
    a_log,
    d_skip,
    out_weight,
    prompt_state,
    prompt_of,
    out_grad,
):
    row_count, width_local = ssm_input.shape
    resp_local = prompt_of.shape[0]
    span_len = row_count // resp_local
    heads = step_size.shape[1]
    groups = b_proj.shape[1] // NS
    per_group = heads // groups
    head_size = width_local // heads
    prompts_local = prompt_state.shape[0]
    bit_count = FAN.bit_length() - 1
    bit_list = list(range(bit_count))
    whole_weight = lax.all_gather(out_weight, "resp", axis=0, tiled=True)
    device = lax.axis_index("resp")
    held_states = prompt_state
    held_ids = device * prompts_local + jnp.arange(prompts_local, dtype=jnp.int32)
    for bit_number in bit_list:
        held_states = jnp.concatenate([held_states, swap_states(held_states, bit_number)], axis=0)
        owners = held_ids // prompts_local
        partner_ids = (
            jnp.bitwise_xor(owners, 1 << bit_number) * prompts_local + held_ids % prompts_local
        )
        held_ids = jnp.concatenate([held_ids, partner_ids])
    selector = (prompt_of[:, None] == held_ids[None, :]).astype(jnp.bfloat16)
    initial = jnp.einsum(
        "rk,khpn->rhpn", selector, held_states, preferred_element_type=jnp.float32
    ).astype(jnp.bfloat16)
    a_negative = -jnp.exp(a_log)
    x_blocks = ssm_input.reshape(resp_local, span_len, groups, per_group, head_size)
    b_blocks = b_proj.reshape(resp_local, span_len, groups, NS)
    c_blocks = c_proj.reshape(resp_local, span_len, groups, NS)
    scores = jnp.einsum("rtgn,rsgn->rgts", c_blocks, b_blocks, preferred_element_type=jnp.float32)
    steps_local = step_size.reshape(resp_local, span_len, heads)
    cumulative = jnp.cumsum(steps_local * a_negative[None, None, :], axis=1)
    cum_heads = jnp.transpose(
        cumulative.reshape(resp_local, span_len, groups, per_group), (0, 2, 3, 1)
    )
    step_heads = jnp.transpose(
        steps_local.reshape(resp_local, span_len, groups, per_group), (0, 2, 3, 1)
    )
    square = span_len * span_len
    cum_later = jnp.repeat(cum_heads, span_len, axis=3)
    cum_earlier = jnp.tile(cum_heads, (1, 1, 1, span_len))
    step_earlier = jnp.tile(step_heads, (1, 1, 1, span_len))
    flat_pos = jnp.arange(square, dtype=jnp.int32)
    causal = flat_pos // span_len >= flat_pos % span_len
    differ = cum_later - cum_earlier
    decays = jnp.where(causal, jnp.exp(jnp.where(causal, differ, 0.0)), 0.0)
    scores_flat = scores.reshape(resp_local, groups, 1, square)
    mixing_flat = (decays * step_earlier * scores_flat).astype(jnp.bfloat16)
    mixing = mixing_flat.reshape(resp_local, groups, per_group, span_len, span_len)
    within = jnp.einsum("rghts,rsghp->rtghp", mixing, x_blocks, preferred_element_type=jnp.float32)
    growth = jnp.exp(cumulative).reshape(resp_local, span_len, groups, per_group)
    init_blocks = initial.reshape(resp_local, groups, per_group, head_size, NS)
    carried = (
        jnp.einsum("rghpn,rtgn->rtghp", init_blocks, c_blocks, preferred_element_type=jnp.float32)
        * growth[..., None]
    )
    skip_gain = d_skip.reshape(groups, per_group)[:, :, None]
    ssm_out = (
        (carried + within + skip_gain * x_blocks)
        .astype(jnp.bfloat16)
        .reshape(row_count, width_local)
    )
    partial_value = jnp.dot(ssm_out, whole_weight, preferred_element_type=jnp.float32)
    mixed = lax.psum_scatter(partial_value, "head", scatter_dimension=0, tiled=True)
    layer_out = mixed.astype(jnp.bfloat16)
    back_grad = jnp.einsum(
        "td,ed->te",
        lax.all_gather(out_grad, "head", axis=0, tiled=True),
        whole_weight,
        preferred_element_type=jnp.float32,
    ).astype(jnp.bfloat16)
    back_blocks = back_grad.reshape(resp_local, span_len, groups, per_group, head_size)
    grad_local = (
        jnp.einsum("rghts,rtghp->rsghp", mixing, back_blocks, preferred_element_type=jnp.float32)
        + skip_gain * back_blocks
    )
    grad_input = grad_local.astype(jnp.bfloat16).reshape(row_count, width_local)
    scaled = (growth[..., None] * back_blocks).astype(jnp.bfloat16)
    group_base = device // FAN * FAN * prompts_local
    slot_index = prompt_of - group_base
    slot_select = (
        jnp.arange(FAN * prompts_local, dtype=jnp.int32)[:, None] == slot_index[None, :]
    ).astype(jnp.bfloat16)
    c_selected = slot_select[:, :, None, None, None] * c_blocks[None]
    per_prompt = jnp.einsum(
        "rtghp,krtgn->kghpn", scaled, c_selected, preferred_element_type=jnp.float32
    )
    blocks = per_prompt.reshape((2,) * bit_count + (prompts_local, heads, head_size, NS))
    done_bits = []
    offset = device % FAN
    for bit_number in bit_list:
        axis_place = len(
            [
                other_bit
                for other_bit in range(bit_count)
                if other_bit > bit_number and other_bit not in done_bits
            ]
        )
        done_bits = done_bits + [bit_number]
        my_half = offset // (1 << bit_number) % 2
        kept_half = lax.dynamic_index_in_dim(blocks, my_half, axis_place, keepdims=False)
        sent_half = lax.dynamic_index_in_dim(blocks, 1 - my_half, axis_place, keepdims=False)
        blocks = kept_half + swap_grads(sent_half, bit_number)
    return (layer_out, grad_input, blocks)


def solution(mesh):
    placed = (
        P("resp", "head"),
        P("resp", "head"),
        P("resp", "head"),
        P("resp", "head"),
        P("head"),
        P("head"),
        P(("head", "resp"), None),
        P("resp", "head", None, None),
        P("resp"),
        P(("resp", "head"), None),
    )
    return jax.shard_map(
        per_device,
        mesh=mesh,
        in_specs=placed,
        out_specs=(P(("resp", "head"), None), P("resp", "head"), P("resp", "head", None, None)),
        check_vma=False,
    )
```

profile of v0, /device:TPU:17, one launch (start us, length us, event | category | flops | bytes accessed | tf_op | source)
XLA Modules:
  0.0 347.8 jit_solution(13034158898531446809)
XLA Ops:
  7.2 0.7 all-gather.3.cloned.1.call-update
  8.0 3.1 collective-permute-start
  11.1 6.2 %collective-permute-done = bf16[1,16,64,128]{3,2,1,0:T(8,128)(2,1)S(1)} collective-permute-done((bf16[1,16,64,128]{3,2,1,0:T(8,128)(2,1)}, bf16[1,16,64,128]{3,2,1,0:T(8,128)(2,1)S(1)}, u32[]{:S(2)}, u32[]{:S(2)}) %collective-permute-start) | collective-permute-done | bytes 262176 | tf_op jit(solution)/shard_map/ppermute | solution.py:11
  17.3 1.8 pad_maximum_fusion.2
  19.0 4.6 %collective-permute-start.1 = (bf16[2,16,64,128]{3,2,1,0:T(8,128)(2,1)}, bf16[2,16,64,128]{3,2,1,0:T(8,128)(2,1)}, u32[]{:S(2)}, u32[]{:S(2)}) collective-permute-start(bf16[2,16,64,128]{3,2,1,0:T(8,128)(2,1)} %pad_maximum_fusion.2), channel_id=1, source_target_pairs={{0,16},{8,24},{16,0},{24,8},{32,48},{40,56},{48,32},{56,40},{64,80... | collective-permute-start | bytes 1572872 | tf_op jit(solution)/shard_map/ppermute | solution.py:11
  23.8 2.6 reshape.188
  26.4 1.3 reshape.183
  27.7 0.8 reshape.180
  28.5 1.5 reshape_reshape.3
  30.0 5.6 %copy.28 = f32[8,64,1,16,64]{1,4,3,0,2:T(8,128)} copy(f32[8,64,1,16,64]{4,3,1,0,2:T(8,128)} %reshape.188) | data formatting | bytes 4194304 | tf_op jit(solution)/shard_map/convert_element_type | solution.py:92
  35.8 2.1 pad_maximum_fusion.1
  37.9 5.8 %collective-permute-start.2 = (bf16[4,16,64,128]{3,2,1,0:T(8,128)(2,1)}, bf16[4,16,64,128]{3,2,1,0:T(8,128)(2,1)}, u32[]{:S(2)}, u32[]{:S(2)}) collective-permute-start(bf16[4,16,64,128]{3,2,1,0:T(8,128)(2,1)} %pad_maximum_fusion.1), channel_id=1, source_target_pairs={{0,32},{8,40},{16,48},{24,56},{32,0},{40,8},{48,16},{56,24},{64,96... | collective-permute-start | bytes 3145736 | tf_op jit(solution)/shard_map/ppermute | solution.py:11
  44.0 0.9 copy.25
  45.3 1.1 fusion.31
  46.4 49.1 %collective-permute-done.2 = bf16[4,16,64,128]{3,2,1,0:T(8,128)(2,1)} collective-permute-done((bf16[4,16,64,128]{3,2,1,0:T(8,128)(2,1)}, bf16[4,16,64,128]{3,2,1,0:T(8,128)(2,1)}, u32[]{:S(2)}, u32[]{:S(2)}) %collective-permute-start.2) | collective-permute-done | bytes 1048608 | tf_op jit(solution)/shard_map/ppermute | solution.py:11
  95.5 1.6 pad_maximum_fusion
  97.1 1.3 fusion.6
  98.4 0.7 fusion.3
  99.2 1.5 copy-done.4
  100.6 4.5 %fusion.2 = bf16[8,64,1,16,64]{1,4,3,0,2:T(8,128)(2,1)} fusion(f32[8,16,64,64]{3,2,1,0:T(8,128)S(1)} %fusion.3, f32[8,64,1,16,64]{1,4,3,0,2:T(8,128)S(1)} %copy-done.4, bf16[8,64,16,64]{3,2,1,0:T(8,128)(2,1)S(1)} %reshape.183, f32[16]{0:T(128)S(1)} %copy-done.17, f32[8,64,16]{1,2,0:T(8,128)S(1)} %copy.22, f32[8,64,64]{2,1,0:T(8,128)S(1)} %fusion.31, ...), kind=kOutput, calls=%fused_computation.4 | convolution fusion | flops 72876032 | bytes 6524992 | tf_op jit(solution)/shard_map/rghts,rsghp->rtghp/dot_general | solution.py:83
  105.1 3.6 %copy.29 = bf16[8,64,1,16,64]{4,3,1,0,2:T(8,128)(2,1)S(1)} copy(bf16[8,64,1,16,64]{1,4,3,0,2:T(8,128)(2,1)} %fusion.2) | data formatting | bytes 2097152 | tf_op jit(solution)/shard_map/convert_element_type | solution.py:93
  108.7 1.5 reshape.184
  110.2 61.0 %all-gather.3.cloned.1.call-done = bf16[1024,2048]{1,0:T(8,128)(2,1)} async-done(((bf16[16,2048]{1,0:T(8,128)(2,1)}), bf16[1024,2048]{1,0:T(8,128)(2,1)}) %all-gather.3.cloned.1.call-update) | async-done | bytes 4194320 | tf_op jit(solution)/shard_map/all_gather | solution.py:44
  171.2 6.5 %fusion.32 = f32[512,2048]{1,0:T(8,128)} fusion(bf16[512,1024]{1,0:T(8,128)(2,1)S(1)} %reshape.184, bf16[1024,2048]{1,0:T(8,128)(2,1)} %all-gather.3.cloned.1.call-done), kind=kOutput, calls=%fused_computation.58 | convolution fusion | flops 2147483648 | bytes 9437184 | tf_op jit(solution)/shard_map/dot_general | solution.py:96
  177.8 33.0 %all-gather.5.cloned.1.call-done = bf16[512,2048]{1,0:T(8,128)(2,1)} async-done(((bf16[64,2048]{1,0:T(8,128)(2,1)}), bf16[512,2048]{1,0:T(8,128)(2,1)}) %all-gather.5.cloned.1.call-update) | async-done | bytes 2097168 | tf_op jit(solution)/shard_map/all_gather | solution.py:101
  210.8 5.2 %convolution_convert_fusion = bf16[512,1024]{1,0:T(8,128)(2,1)S(1)} fusion(bf16[512,2048]{1,0:T(8,128)(2,1)} %all-gather.5.cloned.1.call-done, bf16[1024,2048]{1,0:T(8,128)(2,1)} %all-gather.3.cloned.1.call-done), kind=kOutput, calls=%fused_computation.19 | convolution fusion | flops 2148007936 | bytes 7340032 | tf_op jit(solution)/shard_map/td,ed->te/dot_general | solution.py:99
  216.0 1.3 reshape.185
  217.3 3.3 copy.30
  220.7 3.0 fusion.4
  223.8 1.9 copy-done.3
  225.7 3.1 collective-permute-start.3
  228.8 45.2 %collective-permute-done.3 = f32[2,2,1,16,64,128]{5,4,3,1,0,2:T(8,128)} collective-permute-done((f32[2,2,1,16,64,128]{5,4,3,1,0,2:T(8,128)S(1)}, f32[2,2,1,16,64,128]{5,4,3,1,0,2:T(8,128)}, u32[]{:S(2)}, u32[]{:S(2)}) %collective-permute-start.3) | collective-permute-done | bytes 2097184 | tf_op jit(solution)/shard_map/ppermute | solution.py:11
  274.0 2.6 bitcast_add_fusion.2
  276.6 1.0 dynamic-slice_bitcast_fusion.1
  277.7 4.5 %collective-permute-start.4 = (f32[2,1,16,64,128]{4,3,2,1,0:T(8,128)}, f32[2,1,16,64,128]{4,3,2,1,0:T(8,128)}, u32[]{:S(2)}, u32[]{:S(2)}) collective-permute-start(f32[2,1,16,64,128]{4,3,2,1,0:T(8,128)} %dynamic-slice_bitcast_fusion.1), channel_id=1, source_target_pairs={{0,16},{8,24},{16,0},{24,8},{32,48},{40,56},{48,32},{56,40},{64,80... | collective-permute-start | bytes 3145736 | tf_op jit(solution)/shard_map/ppermute | solution.py:11
  282.3 2.6 reshape.189
  284.9 5.7 %copy.31 = f32[8,64,1,16,64]{1,4,3,0,2:T(8,128)} copy(f32[8,64,1,16,64]{4,3,1,0,2:T(8,128)} %reshape.189) | data formatting | bytes 4194304 | tf_op jit(solution)/shard_map/convert_element_type | solution.py:108
  290.5 15.8 %collective-permute-done.4 = f32[2,1,16,64,128]{4,3,2,1,0:T(8,128)} collective-permute-done((f32[2,1,16,64,128]{4,3,2,1,0:T(8,128)}, f32[2,1,16,64,128]{4,3,2,1,0:T(8,128)}, u32[]{:S(2)}, u32[]{:S(2)}) %collective-permute-start.4) | collective-permute-done | bytes 1048608 | tf_op jit(solution)/shard_map/ppermute | solution.py:11
  306.4 1.4 bitcast_add_fusion.3
  307.8 1.1 copy-done.6
  308.8 0.8 dynamic-slice_bitcast_fusion.2
  309.6 3.8 %collective-permute-start.5 = (f32[1,16,64,128]{3,2,1,0:T(8,128)}, f32[1,16,64,128]{3,2,1,0:T(8,128)}, u32[]{:S(2)}, u32[]{:S(2)}) collective-permute-start(f32[1,16,64,128]{3,2,1,0:T(8,128)} %dynamic-slice_bitcast_fusion.2), channel_id=1, source_target_pairs={{0,32},{8,40},{16,48},{24,56},{32,0},{40,8},{48,16},{56,24},{64,96... | collective-permute-start | bytes 1572872 | tf_op jit(solution)/shard_map/ppermute | solution.py:11
  313.5 4.1 %fusion = bf16[8,64,1,16,64]{1,4,3,0,2:T(8,128)(2,1)} fusion(f32[8,64,1,16,64]{1,4,3,0,2:T(8,128)S(1)} %copy-done.5, bf16[8,64,16,64]{1,3,2,0:T(8,128)(2,1)} %copy.30, f32[16]{0:T(128)S(1)} %copy-done.17, f32[8,64,64]{2,1,0:T(8,128)S(1)} %fusion.31, f32[8,16,64]{2,1,0:T(8,128)S(1)} %copy-done.14, f32[8,16,64]{2,1,0:T(8,128)S(1)} %copy-done.11, ...), kind=kOutput, calls=%fused_computation.1 | convolution fusion | flops 71827456 | bytes 4395072 | tf_op jit(solution)/shard_map/rghts,rtghp->rsghp/dot_general | solution.py:107
  317.6 3.7 %copy.32 = bf16[8,64,1,16,64]{4,3,1,0,2:T(8,128)(2,1)S(1)} copy(bf16[8,64,1,16,64]{1,4,3,0,2:T(8,128)(2,1)} %fusion) | data formatting | bytes 2097152 | tf_op jit(solution)/shard_map/convert_element_type | solution.py:110
  321.3 2.3 reshape.186
  323.6 14.1 %collective-permute-done.5 = f32[1,16,64,128]{3,2,1,0:T(8,128)} collective-permute-done((f32[1,16,64,128]{3,2,1,0:T(8,128)}, f32[1,16,64,128]{3,2,1,0:T(8,128)}, u32[]{:S(2)}, u32[]{:S(2)}) %collective-permute-start.5) | collective-permute-done | bytes 524320 | tf_op jit(solution)/shard_map/ppermute | solution.py:11
  337.6 1.9 bitcast_add_fusion.4
  339.5 1.8 convert_element_type.75
  (52 shorter events, 1.2 us)
Async XLA Ops:
  7.2 38.1 %copy-start = (bf16[512,128]{1,0:T(8,128)(2,1)S(1)}, bf16[512,128]{1,0:T(8,128)(2,1)}, u32[]{:S(2)}) copy-start(bf16[512,128]{1,0:T(8,128)(2,1)} %param.11) | copy-start | bytes 393220
  7.2 16.6 %copy-start.2 = (bf16[512,1024]{1,0:T(8,128)(2,1)S(1)}, bf16[512,1024]{1,0:T(8,128)(2,1)}, u32[]{:S(2)}) copy-start(bf16[512,1024]{1,0:T(8,128)(2,1)} %param.10) | copy-start | bytes 3145732
  7.2 164.0 %all-gather.3.cloned.1.call-start = ((), (), s32[]{:S(2)}) async-start(), calls=%async_computation.1 | async-start | bytes 4259840 | tf_op jit(solution)/shard_map/all_gather | solution.py:44
  7.9 202.9 %all-gather.5.cloned.1.call-start = ((), (), s32[]{:S(2)}) async-start(), calls=%async_computation.3 | async-start | bytes 2359296 | tf_op jit(solution)/shard_map/all_gather | solution.py:101
  8.0 9.3 %collective-permute-start = (bf16[1,16,64,128]{3,2,1,0:T(8,128)(2,1)}, bf16[1,16,64,128]{3,2,1,0:T(8,128)(2,1)S(1)}, u32[]{:S(2)}, u32[]{:S(2)}) collective-permute-start(bf16[1,16,64,128]{3,2,1,0:T(8,128)(2,1)} %param.17), channel_id=1, source_target_pairs={{0,8},{8,0},{16,24},{24,16},{32,40},{40,32},{48,56},{56,48},{64,72... | collective-permute-start | bytes 786440 | tf_op jit(solution)/shard_map/ppermute | solution.py:11
  19.0 16.7 %collective-permute-start.1 = (bf16[2,16,64,128]{3,2,1,0:T(8,128)(2,1)}, bf16[2,16,64,128]{3,2,1,0:T(8,128)(2,1)}, u32[]{:S(2)}, u32[]{:S(2)}) collective-permute-start(bf16[2,16,64,128]{3,2,1,0:T(8,128)(2,1)} %pad_maximum_fusion.2), channel_id=1, source_target_pairs={{0,16},{8,24},{16,0},{24,8},{32,48},{40,56},{48,32},{56,40},{64,80... | collective-permute-start | bytes 1572872 | tf_op jit(solution)/shard_map/ppermute | solution.py:11
  23.7 315.8 %reduce-scatter.2.cloned.1.call-start = ((), (), s32[]{:S(2)}) async-start(), calls=%async_computation.2 | async-start | bytes 4718592 | tf_op jit(solution)/shard_map/reduce_scatter | solution.py:97
  30.0 5.8 %copy-start.8 = (bf16[1,16,64,128]{3,2,1,0:T(8,128)(2,1)S(1)}, bf16[1,16,64,128]{3,2,1,0:T(8,128)(2,1)}, u32[]{:S(2)}) copy-start(bf16[1,16,64,128]{3,2,1,0:T(8,128)(2,1)} %param.17) | copy-start | bytes 786436
  35.6 8.1 %copy-start.16 = (f32[16]{0:T(128)S(1)}, f32[16]{0:T(128)}, u32[]{:S(2)}) copy-start(f32[16]{0:T(128)} %param.14) | copy-start | bytes 196
  37.9 57.6 %collective-permute-start.2 = (bf16[4,16,64,128]{3,2,1,0:T(8,128)(2,1)}, bf16[4,16,64,128]{3,2,1,0:T(8,128)(2,1)}, u32[]{:S(2)}, u32[]{:S(2)}) collective-permute-start(bf16[4,16,64,128]{3,2,1,0:T(8,128)(2,1)} %pad_maximum_fusion.1), channel_id=1, source_target_pairs={{0,32},{8,40},{16,48},{24,56},{32,0},{40,8},{48,16},{56,24},{64,96... | collective-permute-start | bytes 3145736 | tf_op jit(solution)/shard_map/ppermute | solution.py:11
  43.9 55.2 %copy-start.12 = (f32[8,64,16]{1,2,0:T(8,128)}, f32[8,64,16]{1,2,0:T(8,128)S(1)}, u32[]{:S(2)}) copy-start(f32[8,64,16]{1,2,0:T(8,128)S(1)} %copy.22) | copy-start | bytes 98308
  44.8 54.3 %copy-start.13 = (f32[8,16,64]{2,1,0:T(8,128)}, f32[8,16,64]{2,1,0:T(8,128)S(1)}, u32[]{:S(2)}) copy-start(f32[8,16,64]{2,1,0:T(8,128)S(1)} %copy.25) | copy-start | bytes 98308
  45.0 54.2 %copy-start.10 = (f32[8,16,64]{2,1,0:T(8,128)}, f32[8,16,64]{2,1,0:T(8,128)S(1)}, u32[]{:S(2)}) copy-start(f32[8,16,64]{2,1,0:T(8,128)S(1)} %copy.23) | copy-start | bytes 98308
  46.4 50.7 %copy-start.15 = (s32[8]{0:T(128)S(1)}, s32[8]{0:T(128)}, u32[]{:S(2)}) copy-start(s32[8]{0:T(128)} %param.18) | copy-start | bytes 100
  97.1 1.4 copy-start.9
  98.4 2.2 copy-start.4
  98.4 2.2 copy-start.17
  223.6 2.0 copy-start.3
  225.7 48.4 %collective-permute-start.3 = (f32[2,2,1,16,64,128]{5,4,3,1,0,2:T(8,128)S(1)}, f32[2,2,1,16,64,128]{5,4,3,1,0,2:T(8,128)}, u32[]{:S(2)}, u32[]{:S(2)}) collective-permute-start(f32[2,2,1,16,64,128]{5,4,3,1,0,2:T(8,128)S(1)} %dynamic-slice_bitcast_fusion), channel_id=1, source_target_pairs={{0,8},{8,0},{16,24},{24,16},{32,40},{40,32},{48,56},{56,48},{64,72... | collective-permute-start | bytes 6291464 | tf_op jit(solution)/shard_map/ppermute | solution.py:11
  277.7 28.7 %collective-permute-start.4 = (f32[2,1,16,64,128]{4,3,2,1,0:T(8,128)}, f32[2,1,16,64,128]{4,3,2,1,0:T(8,128)}, u32[]{:S(2)}, u32[]{:S(2)}) collective-permute-start(f32[2,1,16,64,128]{4,3,2,1,0:T(8,128)} %dynamic-slice_bitcast_fusion.1), channel_id=1, source_target_pairs={{0,16},{8,24},{16,0},{24,8},{32,48},{40,56},{48,32},{56,40},{64,80... | collective-permute-start | bytes 3145736 | tf_op jit(solution)/shard_map/ppermute | solution.py:11
  284.8 28.6 %copy-start.11 = (f32[8,16,64]{2,1,0:T(8,128)S(1)}, f32[8,16,64]{2,1,0:T(8,128)}, u32[]{:S(2)}) copy-start(f32[8,16,64]{2,1,0:T(8,128)} %copy-done.10) | copy-start | bytes 98308
  284.9 28.6 %copy-start.14 = (f32[8,16,64]{2,1,0:T(8,128)S(1)}, f32[8,16,64]{2,1,0:T(8,128)}, u32[]{:S(2)}) copy-start(f32[8,16,64]{2,1,0:T(8,128)} %copy-done.13) | copy-start | bytes 98308
  290.5 22.9 %copy-start.5 = (f32[8,64,1,16,64]{1,4,3,0,2:T(8,128)S(1)}, f32[8,64,1,16,64]{1,4,3,0,2:T(8,128)}, u32[]{:S(2)}) copy-start(f32[8,64,1,16,64]{1,4,3,0,2:T(8,128)} %copy.31) | copy-start | bytes 6291460
  307.8 1.1 copy-start.6
  309.6 28.0 %collective-permute-start.5 = (f32[1,16,64,128]{3,2,1,0:T(8,128)}, f32[1,16,64,128]{3,2,1,0:T(8,128)}, u32[]{:S(2)}, u32[]{:S(2)}) collective-permute-start(f32[1,16,64,128]{3,2,1,0:T(8,128)} %dynamic-slice_bitcast_fusion.2), channel_id=1, source_target_pairs={{0,32},{8,40},{16,48},{24,56},{32,0},{40,8},{48,16},{56,24},{64,96... | collective-permute-start | bytes 1572872 | tf_op jit(solution)/shard_map/ppermute | solution.py:11
  317.6 23.7 %copy-start.1 = (bf16[512,128]{1,0:T(8,128)(2,1)S(1)}, bf16[512,128]{1,0:T(8,128)(2,1)}, u32[]{:S(2)}) copy-start(bf16[512,128]{1,0:T(8,128)(2,1)} %param.11) | copy-start | bytes 393220
  321.3 16.4 %copy-start.7 = (f32[2,1,16,64,128]{4,3,2,1,0:T(8,128)S(1)}, f32[2,1,16,64,128]{4,3,2,1,0:T(8,128)}, u32[]{:S(2)}) copy-start(f32[2,1,16,64,128]{4,3,2,1,0:T(8,128)} %copy-done.6) | copy-start | bytes 3145732
Sparse Core Ops, SparseCore 0:
  12.5 158.6 all-gather.2
  173.3 37.4 all-gather.4
  213.6 58.9 reduce-scatter.1
where the time goes:
time: 349 us; the launch traced here: 348 us
  waiting for transfers between devices  225 us (64%)
  local copies, waits for them, and re-layouts  43.5 us (12%)
  matrix products  26.3 us (8%)
  starting transfers between devices  25.1 us (7%)
  between operations  14.3 us (4%)
  other arithmetic  13.5 us (4%)
    ppermute x6, waiting for transfers between devices, partner(): lax.ppermute(shard, axis, [(i, i ^ 1 << apart) for i in range(lax.axis_si...  130 us
    all_gather x1, waiting for transfers between devices, per_device(): whole_weight = lax.all_gather(out_weight, 'resp', axis=0, tiled=True)  61 us
    all_gather x1, waiting for transfers between devices, per_device(): lax.all_gather(out_grad, 'head', axis=0, tiled=True)  33 us
    ppermute x6, starting transfers between devices, partner(): lax.ppermute(shard, axis, [(i, i ^ 1 << apart) for i in range(lax.axis_si...  25 us
    convert_element_type x2, local copies, waits for them, and re-layouts, per_device(): skip_gain * back_blocks  8.26 us
    convert_element_type x2, local copies, waits for them, and re-layouts, per_device(): skip_gain * x_blocks  8.17 us
  transfers between devices with their start and end apart: 9, of which 7 were waited for; matrix products, arithmetic and copies ran while one was open for 22% of the time, Pallas kernels for 0%

commit v1 on v0

v1 whole, which is shorter than its diff:
```python
import functools

import jax
import jax.numpy as jnp
from jax import lax
from jax.experimental import pallas as pl
from jax.experimental.pallas import tpu as pltpu
from jax.sharding import PartitionSpec as P

MESH = pl.DeviceIdType.MESH
F32 = jnp.float32
BF16 = jnp.bfloat16
HIGHEST = lax.Precision.HIGHEST

NX, NYH, NZ, NYL, NCORE = 4, 2, 8, 4, 2
GROUP = NX * NYH
RESP_ROWS = 64
RESPS = 8
ROWS = RESP_ROWS * RESPS
NS = 128
HEADS = 16
WIDTH = 1024
DW = 2048
SHARD = 16
LANE = 128
PAIRS = WIDTH // LANE
NBLK = 4
BLK = DW // NBLK


def dot_nt(a, b):
    return lax.dot_general(a, b, (((1,), (1,)), ((), ())), preferred_element_type=F32)


def dot_tn(a, b):
    return lax.dot_general(a, b, (((0,), (0,)), ((), ())), preferred_element_type=F32)


def chunk_of(z, s):
    far = (s + 1) // 2
    sign = 1 - 2 * (s % 2)
    return lax.rem(z + NZ + sign * far, NZ)


def kernel(
    prompt_ref,
    x_ref,
    b_ref,
    c_ref,
    step_ref,
    alog_ref,
    skip_ref,
    w_ref,
    state_ref,
    og_ref,
    layer_ref,
    gin_ref,
    gstate_ref,
    w_all,
    og_all,
    states,
    csel,
    mix,
    mix_t,
    growth,
    ssm,
    back,
    p_tmp,
    p_send,
    p_recv,
    r_own,
    r_send,
    r_recv,
    g_tmp,
    g_own,
    g_send,
    g_recv,
    gy_send,
    gy_recv,
    loc_sem,
    wy_s,
    wy_r,
    wx_s,
    wx_r,
    wz_s,
    wz_r,
    sy_s,
    sy_r,
    sx_s,
    sx_r,
    sf_s,
    sf_r,
    oy_s,
    oy_r,
    oc_s,
    oc_r,
    gx_s,
    gx_r,
    gy_s,
    gy_r,
    pp_s,
    pp_r,
    rr_s,
    rr_r,
):
    resp = lax.axis_index("resp")
    head = lax.axis_index("head")
    x = lax.rem(resp, NX)
    yh = lax.rem(resp // NX, NYH)
    z = resp // GROUP
    core = lax.rem(head, NCORE)
    yl = head // NCORE

    def resp_at(z_, yh_, x_):
        return z_ * GROUP + yh_ * NX + x_

    def dev_x(j):
        return (resp_at(z, yh, lax.rem(x + NX + j, NX)), head)

    def dev_z(j):
        return (resp_at(lax.rem(z + NZ + j, NZ), yh, x), head)

    dev_yh = (resp_at(z, 1 - yh, x), head)
    dev_core = (resp, yl * NCORE + 1 - core)

    def dev_yl(j):
        return (resp, lax.rem(yl + NYL + j, NYL) * NCORE + core)

    def send(src, dst, ss, rs, dev):
        copy = pltpu.make_async_remote_copy(
            src_ref=src, dst_ref=dst, send_sem=ss, recv_sem=rs, device_id=dev, device_id_type=MESH
        )
        copy.start()
        return copy

    def landed(dst, ss, rs, dev):
        pltpu.make_async_remote_copy(
            src_ref=dst, dst_ref=dst, send_sem=ss, recv_sem=rs, device_id=dev, device_id_type=MESH
        ).wait_recv()

    pending = []

    barrier = pltpu.get_barrier_semaphore()
    partners = [dev_yh, dev_core, dev_z(1), dev_z(-1)]
    partners += [dev_x(j) for j in (1, 2, 3)] + [dev_yl(j) for j in (1, 2, 3)]
    for dev in partners:
        pl.semaphore_signal(barrier, inc=1, device_id=dev, device_id_type=MESH)
    pl.semaphore_wait(barrier, len(partners))

    def w_rows(z_, yh_, x_):
        return w_all.at[pl.ds(pl.multiple_of(resp_at(z_, yh_, x_) * SHARD, SHARD), SHARD), :]

    def w_half(z_, yh_):
        start = (z_ * NYH + yh_) * (NX * SHARD)
        return w_all.at[pl.ds(pl.multiple_of(start, NX * SHARD), NX * SHARD), :]

    pending.append(send(w_ref, w_rows(z, yh, x), wy_s, wy_r, dev_yh))
    for j in (1, 2, 3):
        pending.append(
            send(w_ref, w_rows(z, yh, x), wx_s.at[0, j - 1], wx_r.at[0, j - 1], dev_x(j))
        )
    my_slot = yh * NX + x
    og_rows = lambda h_: og_all.at[pl.ds(pl.multiple_of(h_ * RESP_ROWS, RESP_ROWS), RESP_ROWS), :]
    local = [
        pltpu.make_async_copy(w_ref, w_rows(z, yh, x), loc_sem.at[0]),
        pltpu.make_async_copy(state_ref, states.at[my_slot], loc_sem.at[1]),
        pltpu.make_async_copy(og_ref, og_rows(head), loc_sem.at[2]),
    ]
    for copy in local:
        copy.start()

    base = (resp // GROUP) * GROUP

    def fill_csel(r, carry):
        rows = pl.ds(pl.multiple_of(r * RESP_ROWS, RESP_ROWS), RESP_ROWS)
        slot = prompt_ref[r] - base
        c_rows = c_ref[rows, :].astype(F32)
        for k in range(GROUP):
            keep = jnp.where(slot == k, 1.0, 0.0).astype(F32)
            csel[rows, k * NS : (k + 1) * NS] = (c_rows * keep).astype(BF16)
        return carry

    lax.fori_loop(0, RESPS, fill_csel, 0)

    row_id = lax.broadcasted_iota(jnp.int32, (RESP_ROWS, LANE), 0)
    lane_id = lax.broadcasted_iota(jnp.int32, (RESP_ROWS, LANE), 1)
    lane_pos = lax.rem(lane_id, RESP_ROWS)
    first = lane_id < RESP_ROWS
    diag = lane_pos == row_id
    earlier = lane_pos <= row_id
    later = lane_pos >= row_id
    tri = (
        lax.broadcasted_iota(jnp.int32, (RESP_ROWS, RESP_ROWS), 0)
        >= lax.broadcasted_iota(jnp.int32, (RESP_ROWS, RESP_ROWS), 1)
    ).astype(F32)
    a_neg = -jnp.exp(alog_ref[...])

    def spread(columns, i):
        return jnp.where(first, columns[:, 2 * i : 2 * i + 1], columns[:, 2 * i + 1 : 2 * i + 2])

    def fill_mix(r, carry):
        rows = pl.ds(pl.multiple_of(r * RESP_ROWS, RESP_ROWS), RESP_ROWS)
        c_rows, b_rows = c_ref[rows, :], b_ref[rows, :]
        steps = step_ref[rows, :]
        cum = lax.dot_general(
            tri, steps * a_neg, (((1,), (0,)), ((), ())),
            precision=HIGHEST, preferred_element_type=F32,
        )
        score = dot_nt(c_rows, jnp.concatenate([b_rows, b_rows], axis=0))
        score_t = dot_nt(b_rows, jnp.concatenate([c_rows, c_rows], axis=0))
        for i in range(PAIRS):
            cols = slice(i * LANE, (i + 1) * LANE)
            cum_i, step_i = spread(cum, i), spread(steps, i)
            cum_row = jnp.sum(jnp.where(diag, cum_i, 0.0), axis=0, keepdims=True)
            step_row = jnp.sum(jnp.where(diag, step_i, 0.0), axis=0, keepdims=True)
            differ = cum_i - cum_row
            decay = jnp.exp(jnp.where(earlier, differ, 0.0))
            mix[rows, cols] = jnp.where(earlier, decay * step_row * score, 0.0).astype(BF16)
            decay_t = jnp.exp(jnp.where(later, -differ, 0.0))
            mix_t[rows, cols] = jnp.where(later, decay_t * step_i * score_t, 0.0).astype(BF16)
            growth[rows, cols] = jnp.exp(cum_i)
        return carry

    block_mask = (
        (lax.broadcasted_iota(jnp.int32, (LANE, LANE), 0) < RESP_ROWS)
        == (lax.broadcasted_iota(jnp.int32, (LANE, LANE), 1) < RESP_ROWS)
    ).astype(F32).astype(BF16)

    def blocks_of(pair):
        return jnp.concatenate([pair, pair], axis=0) * block_mask

    landed(w_rows(z, 1 - yh, x), wy_s, wy_r, dev_yh)
    for j in (1, 2, 3):
        piece = w_rows(z, 1 - yh, x)
        pending.append(send(piece, piece, wx_s.at[1, j - 1], wx_r.at[1, j - 1], dev_x(j)))
    pending.append(send(state_ref, states.at[my_slot], sy_s, sy_r, dev_yh))
    for i, j in enumerate((1, -1)):
        pending.append(
            send(state_ref, states.at[my_slot], sx_s.at[0, i], sx_r.at[0, i], dev_x(j))
        )
    pending.append(send(og_ref, og_rows(head), oc_s.at[0], oc_r.at[0], dev_core))
    for j in (1, 2, 3):
        pending.append(send(og_ref, og_rows(head), oy_s.at[j - 1], oy_r.at[j - 1], dev_yl(j)))

    local[0].wait()
    for j in (1, 2, 3):
        landed(w_rows(z, yh, lax.rem(x + NX - j, NX)), wx_s.at[0, j - 1], wx_r.at[0, j - 1], dev_x(-j))

    def send_z(step, half):
        yh_ = yh if half == 0 else 1 - yh
        for d, sign in enumerate((1, -1)):
            if step == 3 and half != d:
                continue
            piece = w_half(lax.rem(z + NZ - sign * step, NZ), yh_)
            pending.append(
                send(piece, piece, wz_s.at[d, step, half], wz_r.at[d, step, half], dev_z(sign))
            )

    def land_z(step, half):
        yh_ = yh if half == 0 else 1 - yh
        for d, sign in enumerate((1, -1)):
            if step == 3 and half != d:
                continue
            piece = w_half(lax.rem(z + NZ - sign * (step + 1), NZ), yh_)
            landed(piece, wz_s.at[d, step, half], wz_r.at[d, step, half], dev_z(-sign))

    send_z(0, 0)
    for j in (1, 2, 3):
        landed(
            w_rows(z, 1 - yh, lax.rem(x + NX - j, NX)),
            wx_s.at[1, j - 1],
            wx_r.at[1, j - 1],
            dev_x(-j),
        )
    send_z(0, 1)

    lax.fori_loop(0, 4, fill_mix, 0)

    def slot_of(yh_, j):
        return yh_ * NX + lax.rem(x + NX + j, NX)

    landed(states.at[slot_of(1 - yh, 0)], sy_s, sy_r, dev_yh)
    for i, j in enumerate((1, -1)):
        piece = states.at[slot_of(1 - yh, 0)]
        pending.append(send(piece, piece, sx_s.at[1, i], sx_r.at[1, i], dev_x(j)))

    def pass_states(n, yh_):
        for i, j in enumerate((1, -1)):
            landed(states.at[slot_of(yh_, -j)], sx_s.at[n, i], sx_r.at[n, i], dev_x(-j))
            piece = states.at[slot_of(yh_, -j), pl.ds(i * (WIDTH // 2), WIDTH // 2), :]
            pending.append(send(piece, piece, sf_s.at[n, i], sf_r.at[n, i], dev_x(j)))

    pass_states(0, yh)
    lax.fori_loop(4, RESPS, fill_mix, 0)

    for half in (0, 1):
        land_z(0, half)
        send_z(1, half)

    pass_states(1, 1 - yh)

    local[2].wait()
    landed(og_rows(yl * NCORE + 1 - core), oc_s.at[0], oc_r.at[0], dev_core)
    for j in (1, 2, 3):
        piece = og_rows(lax.rem(yl + NYL - j, NYL) * NCORE + core)
        landed(piece, oy_s.at[j - 1], oy_r.at[j - 1], dev_yl(-j))
        pending.append(send(piece, piece, oc_s.at[j], oc_r.at[j], dev_core))

    local[1].wait()
    for n, yh_ in enumerate((yh, 1 - yh)):
        for i, j in enumerate((1, -1)):
            piece = states.at[slot_of(yh_, 2), pl.ds(i * (WIDTH // 2), WIDTH // 2), :]
            landed(piece, sf_s.at[n, i], sf_r.at[n, i], dev_x(-j))

    for half in (0, 1):
        land_z(1, half)
        send_z(2, half)

    def spread_row(row_ref, i):
        row = row_ref[...]
        where_first = lax.broadcasted_iota(jnp.int32, (1, LANE), 1) < RESP_ROWS
        out = jnp.zeros((1, LANE), F32)
        for h in range(HEADS):
            keep = jnp.where(h // 2 == i, 1.0, 0.0).astype(F32)
            mine = where_first if h % 2 == 0 else jnp.logical_not(where_first)
            out = out + jnp.where(mine, row[:, h : h + 1] * keep, 0.0)
        return out

    def forward(i, carry):
        cols = pl.ds(pl.multiple_of(i * LANE, LANE), LANE)
        skip = spread_row(skip_ref, i)
        init = jnp.concatenate([states[k, cols, :] for k in range(GROUP)], axis=1)
        carried = dot_nt(csel[...], init) * growth[:, cols]
        for r in range(RESPS):
            rows = slice(r * RESP_ROWS, (r + 1) * RESP_ROWS)
            x_rows = x_ref[rows, cols]
            within = jnp.dot(
                mix[rows, cols], blocks_of(x_rows), preferred_element_type=F32
            )
            ssm[rows, cols] = (carried[rows, :] + within + skip * x_rows.astype(F32)).astype(BF16)
        return carry

    lax.fori_loop(0, PAIRS, forward, 0)

    for j in (1, 2, 3):
        piece = og_rows(lax.rem(yl + NYL - j, NYL) * NCORE + 1 - core)
        landed(piece, oc_s.at[j], oc_r.at[j], dev_core)

    def g_piece(ref, j, s):
        return ref.at[j - 1, s]

    def backward(s, carry):
        start = chunk_of(z, s) * LANE
        span = pl.ds(pl.multiple_of(start, LANE), LANE)
        back_f = dot_nt(og_all[...], w_all[span, :])
        back_b = back_f.astype(BF16)
        back[:, span] = back_b
        scaled = (growth[:, span] * back_b.astype(F32)).astype(BF16)
        g_tmp[...] = dot_tn(scaled, csel[...])
        for j in range(NX):
            for y in range(NYH):
                k = y * NX + lax.rem(x + j, NX)
                part = g_tmp[:, pl.ds(pl.multiple_of(k * NS, NS), NS)]
                if j == 0:
                    g_own[s, y] = part
                else:
                    g_send[j - 1, s, y] = part.astype(BF16)
            if j > 0:
                send(
                    g_piece(g_send, j, s), g_piece(g_recv, j, s),
                    gx_s.at[j - 1, s], gx_r.at[j - 1, s], dev_x(j),
                )
        return carry

    def add_x(s, carry):
        for j in (1, 2, 3):
            landed(g_piece(g_recv, j, s), gx_s.at[j - 1, s], gx_r.at[j - 1, s], dev_x(-j))
        span = pl.ds(pl.multiple_of(chunk_of(z, s) * LANE, LANE), LANE)

        def total(y):
            return g_own[s, y] + (
                g_recv[0, s, y].astype(F32) + g_recv[1, s, y].astype(F32) + g_recv[2, s, y].astype(F32)
            )

        gy_send[s] = total(1 - yh).astype(BF16)
        send(gy_send.at[s], gy_recv.at[s], gy_s.at[s], gy_r.at[s], dev_yh)
        gstate_ref[span, :] = total(yh)
        return carry

    lax.fori_loop(0, 3, backward, 0)
    for half in (0, 1):
        land_z(2, half)
        send_z(3, half)
    lax.fori_loop(3, 5, backward, 0)
    lax.fori_loop(0, 3, add_x, 0)
    lax.fori_loop(5, 7, backward, 0)
    for half in (0, 1):
        land_z(3, half)

    def project(n, carry):
        cols = pl.ds(pl.multiple_of(n * BLK, BLK), BLK)
        p_tmp[...] = jnp.dot(ssm[...], w_all[:, cols], preferred_element_type=F32)
        for j in range(NYL):
            other = (lax.rem(yl + j, NYL) * NCORE + 1 - core) * RESP_ROWS
            mine = (lax.rem(yl + j, NYL) * NCORE + core) * RESP_ROWS
            dst_row = lax.rem(yl + j, NYL)
            p_send[n, dst_row] = p_tmp[
                pl.ds(pl.multiple_of(other, RESP_ROWS), RESP_ROWS), :
            ].astype(BF16)
            r_own[n, j] = p_tmp[pl.ds(pl.multiple_of(mine, RESP_ROWS), RESP_ROWS), :]
        send(p_send.at[n], p_recv.at[n], pp_s.at[n], pp_r.at[n], dev_core)
        return carry

    def share(n, carry):
        landed(p_recv.at[n], pp_s.at[n], pp_r.at[n], dev_core)
        for j in range(NYL):
            total = r_own[n, j] + p_recv[n, lax.rem(yl + j, NYL)].astype(F32)
            if j == 0:
                r_own[n, 0] = total
            else:
                r_send[j - 1, n] = total.astype(BF16)
                send(
                    r_send.at[j - 1, n], r_recv.at[j - 1, n],
                    rr_s.at[j - 1, n], rr_r.at[j - 1, n], dev_yl(j),
                )
        return carry

    lax.fori_loop(0, NBLK, project, 0)
    lax.fori_loop(0, NBLK, share, 0)
    lax.fori_loop(7, 8, backward, 0)
    lax.fori_loop(3, 8, add_x, 0)

    def input_grad(i, carry):
        cols = pl.ds(pl.multiple_of(i * LANE, LANE), LANE)
        skip = spread_row(skip_ref, i)
        for r in range(RESPS):
            rows = slice(r * RESP_ROWS, (r + 1) * RESP_ROWS)
            b_rows = back[rows, cols]
            within = jnp.dot(
                mix_t[rows, cols], blocks_of(b_rows), preferred_element_type=F32
            )
            gin_ref[rows, cols] = (within + skip * b_rows.astype(F32)).astype(BF16)
        return carry

    lax.fori_loop(0, PAIRS, input_grad, 0)

    def finish_state(s, carry):
        landed(gy_recv.at[s], gy_s.at[s], gy_r.at[s], dev_yh)
        span = pl.ds(pl.multiple_of(chunk_of(z, s) * LANE, LANE), LANE)
        gstate_ref[span, :] = gstate_ref[span, :] + gy_recv[s].astype(F32)
        return carry

    lax.fori_loop(0, NZ, finish_state, 0)

    for n in range(NBLK):
        total = r_own[n, 0]
        for j in (1, 2, 3):
            landed(r_recv.at[j - 1, n], rr_s.at[j - 1, n], rr_r.at[j - 1, n], dev_yl(-j))
            total = total + r_recv[j - 1, n].astype(F32)
        layer_ref[:, n * BLK : (n + 1) * BLK] = total.astype(BF16)

    for copy in pending:
        copy.wait_send()

    def sent(src, dst, ss, rs, dev):
        pltpu.make_async_remote_copy(
            src_ref=src, dst_ref=dst, send_sem=ss, recv_sem=rs, device_id=dev, device_id_type=MESH
        ).wait_send()

    def drain_g(s, carry):
        for j in (1, 2, 3):
            sent(
                g_piece(g_send, j, s), g_piece(g_recv, j, s),
                gx_s.at[j - 1, s], gx_r.at[j - 1, s], dev_x(j),
            )
        sent(gy_send.at[s], gy_recv.at[s], gy_s.at[s], gy_r.at[s], dev_yh)
        return carry

    lax.fori_loop(0, NZ, drain_g, 0)

    def drain_p(n, carry):
        sent(p_send.at[n], p_recv.at[n], pp_s.at[n], pp_r.at[n], dev_core)
        for j in (1, 2, 3):
            sent(
                r_send.at[j - 1, n], r_recv.at[j - 1, n],
                rr_s.at[j - 1, n], rr_r.at[j - 1, n], dev_yl(j),
            )
        return carry

    lax.fori_loop(0, NBLK, drain_p, 0)


def per_device(
    ssm_input,
    b_proj,
    c_proj,
    step_size,
    a_log,
    d_skip,
    out_weight,
    prompt_state,
    prompt_of,
    out_grad,
):
    vmem = pl.BlockSpec(memory_space=pltpu.VMEM)
    anywhere = pl.BlockSpec(memory_space=pl.ANY)
    dma = pltpu.SemaphoreType.DMA
    sems = [
        (),
        (2, 3),
        (2, 4, 2),
        (),
        (2, 2),
        (2, 2),
        (3,),
        (4,),
        (3, NZ),
        (NZ,),
        (NBLK,),
        (3, NBLK),
    ]
    sem_scratch = []
    for shape in sems:
        sem_scratch += [dma(shape), dma(shape)]
    layer_out, grad_input, grad_state = pl.pallas_call(
        kernel,
        out_shape=(
            jax.ShapeDtypeStruct((RESP_ROWS, DW), BF16),
            jax.ShapeDtypeStruct((ROWS, WIDTH), BF16),
            jax.ShapeDtypeStruct((WIDTH, NS), F32),
        ),
        in_specs=[pl.BlockSpec(memory_space=pltpu.SMEM)] + [vmem] * 6 + [anywhere] * 3,
        out_specs=(vmem, vmem, vmem),
        scratch_shapes=[
            pltpu.VMEM((WIDTH, DW), BF16),
            pltpu.VMEM((ROWS, DW), BF16),
            pltpu.VMEM((GROUP, WIDTH, NS), BF16),
            pltpu.VMEM((ROWS, GROUP * NS), BF16),
            pltpu.VMEM((ROWS, WIDTH), BF16),
            pltpu.VMEM((ROWS, WIDTH), BF16),
            pltpu.VMEM((ROWS, WIDTH), F32),
            pltpu.VMEM((ROWS, WIDTH), BF16),
            pltpu.VMEM((ROWS, WIDTH), BF16),
            pltpu.VMEM((ROWS, BLK), F32),
            pltpu.VMEM((NBLK, NYL, RESP_ROWS, BLK), BF16),
            pltpu.VMEM((NBLK, NYL, RESP_ROWS, BLK), BF16),
            pltpu.VMEM((NBLK, NYL, RESP_ROWS, BLK), F32),
            pltpu.VMEM((3, NBLK, RESP_ROWS, BLK), BF16),
            pltpu.VMEM((3, NBLK, RESP_ROWS, BLK), BF16),
            pltpu.VMEM((LANE, GROUP * NS), F32),
            pltpu.VMEM((NZ, NYH, LANE, NS), F32),
            pltpu.VMEM((3, NZ, NYH, LANE, NS), BF16),
            pltpu.VMEM((3, NZ, NYH, LANE, NS), BF16),
            pltpu.VMEM((NZ, LANE, NS), BF16),
            pltpu.VMEM((NZ, LANE, NS), BF16),
            dma((3,)),
        ]
        + sem_scratch,
        compiler_params=pltpu.CompilerParams(
            collective_id=0, has_side_effects=True, vmem_limit_bytes=56 * 1024 * 1024
        ),
        name="ssd_span",
    )(
        prompt_of,
        ssm_input,
        b_proj,
        c_proj,
        step_size,
        a_log.reshape(1, HEADS),
        d_skip.reshape(1, HEADS),
        out_weight,
        prompt_state.reshape(WIDTH, NS),
        out_grad,
    )
    return layer_out, grad_input, grad_state.reshape(1, HEADS, WIDTH // HEADS, NS)


def solution(mesh):
    placed = (
        P("resp", "head"),
        P("resp", "head"),
        P("resp", "head"),
        P("resp", "head"),
        P("head"),
        P("head"),
        P(("head", "resp"), None),
        P("resp", "head", None, None),
        P("resp"),
        P(("resp", "head"), None),
    )
    return jax.shard_map(
        per_device,
        mesh=mesh,
        in_specs=placed,
        out_specs=(P(("resp", "head"), None), P("resp", "head"), P("resp", "head", None, None)),
        check_vma=False,
    )
```

time: 349 us -> 117 us (0.34)
  the two profiles are of different devices: /device:TPU:17 before, /device:TPU:8 now
where the time goes in v1:
time: 117 us
  Pallas kernels  110 us (94%)
  local copies, waits for them, and re-layouts  6.38 us (5%)
    pallas_call x1, Pallas kernels, per_device(): pl.pallas_call(kernel, out_shape=(jax.ShapeDtypeStruct((RESP_ROWS, DW), B...  110 us
    unnamed x6, local copies, waits for them, and re-layouts  6.38 us

profile of v1, /device:TPU:8, one launch (start us, length us, event | category | flops | bytes accessed | tf_op | source)
XLA Modules:
  0.0 117.1 jit_solution(16031581609300835513)
XLA Ops:
  0.6 1.6 %copy.13.step_ref = f32[512,16]{1,0:T(8,128)} copy(f32[512,16]{0,1:T(8,128)} %param.13) | data formatting | bytes 65536 | tf_op args[3]
  2.2 110.1 %ssd_span.1 = (bf16[64,2048]{1,0:T(8,128)(2,1)}, bf16[512,1024]{1,0:T(8,128)(2,1)}, f32[1024,128]{1,0:T(8,128)}) custom-call(s32[8]{0:T(128)} %prompt_ref.1, bf16[512,1024]{1,0:T(8,128)(2,1)} %x_ref.1, bf16[512,128]{1,0:T(8,128)(2,1)} %b_ref.1, bf16[512,128]{1,0:T(8,128)(2,1)} %c_ref.1, f32[512,16]{1,0:T(8,128)} %copy.13.step_ref, f32[1,16]{1,0:T(1,128)} %bitcast.6, ...), custom_call_target="tpu_custom_call" | custom-call | tf_op jit(solution)/shard_map/ssd_span/pallas_call | solution.py:525
  112.3 1.7 %copy.17 = bf16[64,2048]{1,0:T(8,128)(2,1)} copy(bf16[64,2048]{1,0:T(8,128)(2,1)} %get-tuple-element.12) | data formatting | bytes 524288
  114.0 0.0 copy-start
  114.0 2.3 %copy.18 = bf16[512,1024]{1,0:T(8,128)(2,1)} copy(bf16[512,1024]{1,0:T(8,128)(2,1)} %get-tuple-element.13) | data formatting | bytes 2097152
  116.3 0.0 copy-done
  116.3 0.8 copy.19
Async XLA Ops:
  114.0 2.3 %copy-start = (f32[1024,128]{1,0:T(8,128)S(1)}, f32[1024,128]{1,0:T(8,128)}, u32[]{:S(2)}) copy-start(f32[1024,128]{1,0:T(8,128)} %get-tuple-element.8) | copy-start | bytes 1572868

commit v2 on v1

v2 whole, which is shorter than its diff:
```python
import functools

import jax
import jax.numpy as jnp
from jax import lax
from jax.experimental import pallas as pl
from jax.experimental.pallas import tpu as pltpu
from jax.sharding import PartitionSpec as P

MESH = pl.DeviceIdType.MESH
F32 = jnp.float32
BF16 = jnp.bfloat16
HIGHEST = lax.Precision.HIGHEST

NX, NYH, NZ, NYL, NCORE = 4, 2, 8, 4, 2
GROUP = NX * NYH
RESP_ROWS = 64
RESPS = 8
ROWS = RESP_ROWS * RESPS
NS = 128
HEADS = 16
WIDTH = 1024
DW = 2048
SHARD = 16
LANE = 128
PAIRS = WIDTH // LANE
NBLK = 4
BLK = DW // NBLK
EARLY = BLK
CUT = 1536


def dot_nt(a, b):
    return lax.dot_general(a, b, (((1,), (1,)), ((), ())), preferred_element_type=F32)


def dot_tn(a, b):
    return lax.dot_general(a, b, (((0,), (0,)), ((), ())), preferred_element_type=F32)


def chunk_of(z, s):
    far = (s + 1) // 2
    sign = 1 - 2 * (s % 2)
    return lax.rem(z + NZ + sign * far, NZ)


def kernel(
    prompt_ref,
    step_ref,
    alog_ref,
    skip_ref,
    x_hbm,
    b_hbm,
    c_hbm,
    w_ref,
    state_ref,
    og_ref,
    layer_ref,
    gin_ref,
    gstate_ref,
    x_ref,
    b_ref,
    c_ref,
    steps_ref,
    w_all,
    w_part,
    og_all,
    states,
    csel,
    inner,
    mix,
    mix_t,
    growth,
    ssm,
    back,
    p_tmp,
    p_send,
    p_recv,
    r_own,
    r_send,
    r_recv,
    g_tmp,
    g_own,
    g_send,
    g_recv,
    gy_send,
    gy_recv,
    loc_sem,
    wy_s,
    wy_r,
    wx_s,
    wx_r,
    wz_s,
    wz_r,
    pz_s,
    pz_r,
    vz_s,
    vz_r,
    vx_s,
    vx_r,
    vf_s,
    vf_r,
    sy_s,
    sy_r,
    sx_s,
    sx_r,
    sf_s,
    sf_r,
    oy_s,
    oy_r,
    oc_s,
    oc_r,
    gx_s,
    gx_r,
    gy_s,
    gy_r,
    pp_s,
    pp_r,
    rr_s,
    rr_r,
):
    resp = lax.axis_index("resp")
    head = lax.axis_index("head")
    x = lax.rem(resp, NX)
    yh = lax.rem(resp // NX, NYH)
    z = resp // GROUP
    core = lax.rem(head, NCORE)
    yl = head // NCORE

    def resp_at(z_, yh_, x_):
        return z_ * GROUP + yh_ * NX + x_

    def x_at(j):
        return lax.rem(x + NX + j, NX)

    def z_at(j):
        return lax.rem(z + NZ + j, NZ)

    def dev_x(j):
        return (resp_at(z, yh, x_at(j)), head)

    def dev_z(j):
        return (resp_at(z_at(j), yh, x), head)

    dev_yh = (resp_at(z, 1 - yh, x), head)
    dev_core = (resp, yl * NCORE + 1 - core)

    def dev_yl(j):
        return (resp, (yl + j) * NCORE + core)

    def send(src, dst, ss, rs, dev):
        copy = pltpu.make_async_remote_copy(
            src_ref=src, dst_ref=dst, send_sem=ss, recv_sem=rs, device_id=dev, device_id_type=MESH
        )
        copy.start()
        return copy

    def landed(dst, ss, rs, dev):
        pltpu.make_async_remote_copy(
            src_ref=dst, dst_ref=dst, send_sem=ss, recv_sem=rs, device_id=dev, device_id_type=MESH
        ).wait_recv()

    def sent(src, dst, ss, rs, dev):
        pltpu.make_async_remote_copy(
            src_ref=src, dst_ref=dst, send_sem=ss, recv_sem=rs, device_id=dev, device_id_type=MESH
        ).wait_send()

    pending = []
    SIGNS = ((0, 1), (1, -1))

    def has(j):
        return yl + j < NYL if j > 0 else yl + j >= 0

    barrier = pltpu.get_barrier_semaphore()
    partners = [dev_yh, dev_core] + [dev_z(j) for j in range(1, NZ)]
    partners += [dev_x(j) for j in range(1, NX)]
    partners += [(resp, lax.rem(yl + j, NYL) * NCORE + core) for j in (1, NYL - 1)]
    for dev in partners:
        pl.semaphore_signal(barrier, inc=1, device_id=dev, device_id_type=MESH)
    local = [
        pltpu.make_async_copy(c_hbm, c_ref, loc_sem.at[0]),
        pltpu.make_async_copy(b_hbm, b_ref, loc_sem.at[1]),
    ]
    for copy in local:
        copy.start()
    pl.semaphore_wait(barrier, len(partners))
    def w_rows(z_, yh_, x_):
        return pl.ds(pl.multiple_of(resp_at(z_, yh_, x_) * SHARD, SHARD), SHARD)

    def w_half(z_, yh_):
        start = (z_ * NYH + yh_) * (NX * SHARD)
        return pl.ds(pl.multiple_of(start, NX * SHARD), NX * SHARD)

    def og_rows(h_):
        return og_all.at[pl.ds(pl.multiple_of(h_ * RESP_ROWS, RESP_ROWS), RESP_ROWS), :]

    w_a, w_b = w_ref.at[:, 0:CUT], w_ref.at[:, CUT:DW]
    own_rows, oth_rows = w_rows(z, yh, x), w_rows(z, 1 - yh, x)
    pending.append(send(w_a, w_all.at[own_rows, 0:CUT], wy_s.at[0], wy_r.at[0], dev_yh))
    pending.append(send(w_b, w_part.at[x, z, yh], wy_s.at[1], wy_r.at[1], dev_yh))
    my_slot = yh * NX + x
    pending.append(send(state_ref, states.at[my_slot], sy_s, sy_r, dev_yh))
    for j in (1, 2, 3):
        pending.append(
            send(w_a, w_all.at[own_rows, 0:CUT], wx_s.at[0, j - 1], wx_r.at[0, j - 1], dev_x(j))
        )

    def send_v(half):
        piece = w_part.at[x, z, yh if half == 0 else 1 - yh]
        for j in range(1, NZ):
            pending.append(
                send(
                    w_b if half == 0 else piece, piece,
                    vz_s.at[half, j - 1], vz_r.at[half, j - 1], dev_z(j),
                )
            )

    def land_v(half):
        for j in range(1, NZ):
            piece = w_part.at[x, z_at(-j), yh if half == 0 else 1 - yh]
            landed(piece, vz_s.at[half, j - 1], vz_r.at[half, j - 1], dev_z(-j))

    send_v(0)

    def send_og(i, d, sign):
        @pl.when(jnp.logical_and(has(sign), has(-sign * i)) if i else has(sign))
        def _():
            piece = og_rows((yl - sign * i) * NCORE + core)
            send(og_ref if i == 0 else piece, piece, oy_s.at[d, i], oy_r.at[d, i], dev_yl(sign))

    def drain_og(i, d, sign):
        @pl.when(jnp.logical_and(has(sign), has(-sign * i)) if i else has(sign))
        def _():
            piece = og_rows((yl - sign * i) * NCORE + core)
            sent(og_ref if i == 0 else piece, piece, oy_s.at[d, i], oy_r.at[d, i], dev_yl(sign))

    def land_og(i):
        for d, sign in SIGNS:

            @pl.when(has(-sign * (i + 1)))
            def _():
                piece = og_rows((yl - sign * (i + 1)) * NCORE + core)
                landed(piece, oy_s.at[d, i], oy_r.at[d, i], dev_yl(-sign))
                send(piece, piece, oc_s.at[1 + 3 * d + i], oc_r.at[1 + 3 * d + i], dev_core)

        if i < 2:
            for d, sign in SIGNS:
                send_og(i + 1, d, sign)

    local += [
        pltpu.make_async_copy(w_a, w_all.at[own_rows, 0:CUT], loc_sem.at[2]),
        pltpu.make_async_copy(w_b, w_part.at[x, z, yh], loc_sem.at[3]),
        pltpu.make_async_copy(og_ref, og_rows(head), loc_sem.at[4]),
        pltpu.make_async_copy(state_ref, states.at[my_slot], loc_sem.at[5]),
        pltpu.make_async_copy(x_hbm, x_ref, loc_sem.at[6]),
    ]
    for copy in local[2:]:
        copy.start()

    base = (resp // GROUP) * GROUP
    steps_ref[...] = jnp.transpose(step_ref[...])

    def fill_csel(r, carry):
        rows = pl.ds(pl.multiple_of(r * RESP_ROWS, RESP_ROWS), RESP_ROWS)
        slot = prompt_ref[r] - base
        c_rows = c_ref[rows, :].astype(F32)
        for k in range(GROUP):
            keep = jnp.where(slot == k, 1.0, 0.0).astype(F32)
            csel[rows, k * NS : (k + 1) * NS] = (c_rows * keep).astype(BF16)
        return carry

    row_id = lax.broadcasted_iota(jnp.int32, (RESP_ROWS, LANE), 0)
    lane_id = lax.broadcasted_iota(jnp.int32, (RESP_ROWS, LANE), 1)
    lane_pos = lax.rem(lane_id, RESP_ROWS)
    first = lane_id < RESP_ROWS
    diag = lane_pos == row_id
    earlier = lane_pos <= row_id
    later = lane_pos >= row_id
    tri = (
        lax.broadcasted_iota(jnp.int32, (RESP_ROWS, RESP_ROWS), 0)
        >= lax.broadcasted_iota(jnp.int32, (RESP_ROWS, RESP_ROWS), 1)
    ).astype(F32)
    a_neg = -jnp.exp(alog_ref[...])

    def spread(columns, i):
        return jnp.where(first, columns[:, 2 * i : 2 * i + 1], columns[:, 2 * i + 1 : 2 * i + 2])

    def fill_mix(r, carry):
        rows = pl.ds(pl.multiple_of(r * RESP_ROWS, RESP_ROWS), RESP_ROWS)
        c_rows, b_rows = c_ref[rows, :], b_ref[rows, :]
        steps = steps_ref[rows, :]
        cum = lax.dot_general(
            tri, steps * a_neg, (((1,), (0,)), ((), ())),
            precision=HIGHEST, preferred_element_type=F32,
        )
        score = dot_nt(c_rows, jnp.concatenate([b_rows, b_rows], axis=0))
        score_t = dot_nt(b_rows, jnp.concatenate([c_rows, c_rows], axis=0))
        for i in range(PAIRS):
            cols = slice(i * LANE, (i + 1) * LANE)
            cum_i, step_i = spread(cum, i), spread(steps, i)
            cum_row = jnp.sum(jnp.where(diag, cum_i, 0.0), axis=0, keepdims=True)
            step_row = jnp.sum(jnp.where(diag, step_i, 0.0), axis=0, keepdims=True)
            differ = cum_i - cum_row
            decay = jnp.exp(jnp.where(earlier, differ, 0.0))
            mix[rows, cols] = jnp.where(earlier, decay * step_row * score, 0.0).astype(BF16)
            decay_t = jnp.exp(jnp.where(later, -differ, 0.0))
            mix_t[rows, cols] = jnp.where(later, decay_t * step_i * score_t, 0.0).astype(BF16)
            growth[rows, cols] = jnp.exp(cum_i)
        return carry

    block_mask = (
        (lax.broadcasted_iota(jnp.int32, (LANE, LANE), 0) < RESP_ROWS)
        == (lax.broadcasted_iota(jnp.int32, (LANE, LANE), 1) < RESP_ROWS)
    ).astype(F32).astype(BF16)

    def blocks_of(pair):
        return jnp.concatenate([pair, pair], axis=0) * block_mask

    def z_pieces(step, half, sent_ones):
        yh_ = yh if half == 0 else 1 - yh
        for d, sign in SIGNS:
            if step == 3 and half != d:
                continue
            z_ = z_at(-sign * (step if sent_ones else step + 1))
            piece = w_all.at[w_half(z_, yh_), EARLY:CUT]
            yield piece, wz_s.at[d, step, half], wz_r.at[d, step, half], sign

    def send_z(step, half):
        for piece, ss, rs, sign in z_pieces(step, half, True):
            pending.append(send(piece, piece, ss, rs, dev_z(sign)))

    def land_z(step, half):
        for piece, ss, rs, sign in z_pieces(step, half, False):
            landed(piece, ss, rs, dev_z(-sign))

    def p_pieces(step, sent_ones):
        for d, sign in SIGNS:
            z_ = z_at(-sign * (step if sent_ones else step + 1))
            if step == 3:
                rows = w_half(z_, yh if d == 0 else 1 - yh)
            else:
                rows = pl.ds(pl.multiple_of(z_ * LANE, LANE), LANE)
            yield w_all.at[rows, 0:EARLY], pz_s.at[d, step], pz_r.at[d, step], sign

    def send_p(step):
        for piece, ss, rs, sign in p_pieces(step, True):
            pending.append(send(piece, piece, ss, rs, dev_z(sign)))

    def land_p(step):
        for piece, ss, rs, sign in p_pieces(step, False):
            landed(piece, ss, rs, dev_z(-sign))

    def slot_of(yh_, j):
        return yh_ * NX + x_at(j)

    def send_states(n):
        yh_ = yh if n == 0 else 1 - yh
        piece = states.at[slot_of(yh_, 0)]
        for d, sign in SIGNS:
            pending.append(
                send(
                    state_ref if n == 0 else piece, piece,
                    sx_s.at[n, d], sx_r.at[n, d], dev_x(sign),
                )
            )

    def pass_states(n):
        yh_ = yh if n == 0 else 1 - yh
        for d, sign in SIGNS:
            landed(states.at[slot_of(yh_, -sign)], sx_s.at[n, d], sx_r.at[n, d], dev_x(-sign))
            piece = states.at[slot_of(yh_, -sign), pl.ds(d * (WIDTH // 2), WIDTH // 2), :]
            pending.append(send(piece, piece, sf_s.at[n, d], sf_r.at[n, d], dev_x(sign)))

    def land_states(n):
        yh_ = yh if n == 0 else 1 - yh
        for d, sign in SIGNS:
            piece = states.at[slot_of(yh_, 2), pl.ds(d * (WIDTH // 2), WIDTH // 2), :]
            landed(piece, sf_s.at[n, d], sf_r.at[n, d], dev_x(-sign))

    def part_half(j, d):
        return w_part.at[x_at(j), pl.ds(d * (NZ // 2), NZ // 2)]

    def spread_row(row_ref, i):
        row = row_ref[...]
        where_first = lax.broadcasted_iota(jnp.int32, (1, LANE), 1) < RESP_ROWS
        out = jnp.zeros((1, LANE), F32)
        for h in range(HEADS):
            keep = jnp.where(h // 2 == i, 1.0, 0.0).astype(F32)
            mine = where_first if h % 2 == 0 else jnp.logical_not(where_first)
            out = out + jnp.where(mine, row[:, h : h + 1] * keep, 0.0)
        return out

    def forward_within(i, carry):
        cols = pl.ds(pl.multiple_of(i * LANE, LANE), LANE)
        skip = spread_row(skip_ref, i)
        for r in range(RESPS):
            rows = slice(r * RESP_ROWS, (r + 1) * RESP_ROWS)
            x_rows = x_ref[rows, cols]
            within = jnp.dot(
                mix[rows, cols], blocks_of(x_rows), preferred_element_type=F32
            )
            inner[rows, cols] = within + skip * x_rows.astype(F32)
        return carry

    def carried(i, yh_):
        cols = pl.ds(pl.multiple_of(i * LANE, LANE), LANE)
        init = jnp.concatenate([states[yh_ * NX + k, cols, :] for k in range(NX)], axis=1)
        mine = csel[:, pl.ds(pl.multiple_of(yh_ * (NX * NS), NX * NS), NX * NS)]
        return cols, dot_nt(mine, init) * growth[:, cols]

    def forward_own(i, carry):
        cols, more = carried(i, yh)
        inner[:, cols] = inner[:, cols] + more
        return carry

    def forward_other(i, carry):
        cols, more = carried(i, 1 - yh)
        ssm[:, cols] = (inner[:, cols] + more).astype(BF16)
        return carry

    def g_piece(ref, j, u):
        return ref.at[j - 1, pl.ds(2 * u, 2)]

    def unpack(z_, carry):
        for yh_ in range(NYH):
            for x_ in range(NX):
                w_all[w_rows(z_, yh_, x_), CUT:DW] = w_part[x_, z_, yh_]
        return carry

    def span_of(s_):
        return pl.ds(pl.multiple_of(chunk_of(z, s_) * LANE, LANE), LANE)

    def backward(u, carry):
        spans = [span_of(2 * u + i) for i in range(2)]
        rows = jnp.concatenate([w_all[span, :] for span in spans], axis=0)
        back_f = dot_nt(og_all[...], rows)
        back_b = back_f.astype(BF16)
        for i in range(2):
            back[:, spans[i]] = back_b[:, i * LANE : (i + 1) * LANE]
        grown = jnp.concatenate([growth[:, span] for span in spans], axis=1)
        scaled = (grown * back_b.astype(F32)).astype(BF16)
        g_tmp[...] = dot_tn(scaled, csel[...])
        for j in range(NX):
            for y in range(NYH):
                k = y * NX + lax.rem(x + j, NX)
                for i in range(2):
                    piece = g_tmp[
                        i * LANE : (i + 1) * LANE, pl.ds(pl.multiple_of(k * NS, NS), NS)
                    ]
                    if j == 0:
                        g_own[2 * u + i, y] = piece
                    else:
                        g_send[j - 1, 2 * u + i, y] = piece.astype(BF16)
            if j > 0:
                send(
                    g_piece(g_send, j, u), g_piece(g_recv, j, u),
                    gx_s.at[j - 1, u], gx_r.at[j - 1, u], dev_x(j),
                )
        return carry

    def add_x(u, carry):
        for j in (1, 2, 3):
            landed(g_piece(g_recv, j, u), gx_s.at[j - 1, u], gx_r.at[j - 1, u], dev_x(-j))

        def total(s_, y):
            return g_own[s_, y] + (
                g_recv[0, s_, y].astype(F32)
                + g_recv[1, s_, y].astype(F32)
                + g_recv[2, s_, y].astype(F32)
            )

        for i in range(2):
            gy_send[2 * u + i] = total(2 * u + i, 1 - yh).astype(BF16)
        two = pl.ds(2 * u, 2)
        send(gy_send.at[two], gy_recv.at[two], gy_s.at[u], gy_r.at[u], dev_yh)
        for i in range(2):
            gstate_ref[span_of(2 * u + i), :] = total(2 * u + i, yh)
        return carry

    def give(n):
        for j in range(NYL):
            p_send[n, j] = p_tmp[
                pl.ds(pl.multiple_of((j * NCORE + 1 - core) * RESP_ROWS, RESP_ROWS), RESP_ROWS), :
            ].astype(BF16)
            r_own[n, j] = p_tmp[
                pl.ds(pl.multiple_of((j * NCORE + core) * RESP_ROWS, RESP_ROWS), RESP_ROWS), :
            ]
        send(p_send.at[n], p_recv.at[n], pp_s.at[n], pp_r.at[n], dev_core)

    def project(n, carry):
        cols = pl.ds(pl.multiple_of(n * BLK, BLK), BLK)
        p_tmp[...] = jnp.dot(ssm[...], w_all[:, cols], preferred_element_type=F32)
        give(n)
        return carry

    def share(n, carry):
        landed(p_recv.at[n], pp_s.at[n], pp_r.at[n], dev_core)
        for j in range(NYL):
            r_own[n, j] = r_own[n, j] + p_recv[n, j].astype(F32)
        return carry

    def chain(n, d):
        sign = 1 - 2 * d

        def here(place):
            return jnp.logical_and(place >= 0, place < NYL)

        for o in (3, 2, 1):

            @pl.when(here(yl + sign * o))
            def _():
                total = r_own[n, yl + sign * o]
                r_send[d, o - 1, n] = total.astype(BF16)
                if o < 3:

                    @pl.when(here(yl - sign))
                    def _():
                        landed(
                            r_recv.at[d, o, n], rr_s.at[d, o, n], rr_r.at[d, o, n], dev_yl(-sign)
                        )
                        r_send[d, o - 1, n] = (total + r_recv[d, o, n].astype(F32)).astype(BF16)

                send(
                    r_send.at[d, o - 1, n], r_recv.at[d, o - 1, n],
                    rr_s.at[d, o - 1, n], rr_r.at[d, o - 1, n], dev_yl(sign),
                )

    def finish_layer(n, carry):
        for d, sign in SIGNS:

            @pl.when(has(-sign))
            def _():
                landed(r_recv.at[d, 0, n], rr_s.at[d, 0, n], rr_r.at[d, 0, n], dev_yl(-sign))
                r_own[n, yl] = r_own[n, yl] + r_recv[d, 0, n].astype(F32)

        layer_ref[:, pl.ds(pl.multiple_of(n * BLK, BLK), BLK)] = r_own[n, yl].astype(BF16)
        return carry

    def input_grad(i, carry):
        cols = pl.ds(pl.multiple_of(i * LANE, LANE), LANE)
        skip = spread_row(skip_ref, i)
        for r in range(RESPS):
            rows = slice(r * RESP_ROWS, (r + 1) * RESP_ROWS)
            b_rows = back[rows, cols]
            within = jnp.dot(
                mix_t[rows, cols], blocks_of(b_rows), preferred_element_type=F32
            )
            gin_ref[rows, cols] = (within + skip * b_rows.astype(F32)).astype(BF16)
        return carry

    def finish_state(u, carry):
        two = pl.ds(2 * u, 2)
        landed(gy_recv.at[two], gy_s.at[u], gy_r.at[u], dev_yh)
        for i in range(2):
            span = span_of(2 * u + i)
            gstate_ref[span, :] = gstate_ref[span, :] + gy_recv[2 * u + i].astype(F32)
        return carry

    def run(body, *indices):
        lax.fori_loop(indices[0], indices[-1] + 1, body, 0)

    near = yl // (NYL // 2)

    local[0].wait()
    local[1].wait()
    run(fill_mix, 0, 2)
    landed(w_all.at[oth_rows, 0:CUT], wy_s.at[0], wy_r.at[0], dev_yh)
    for j in (1, 2, 3):
        piece = w_all.at[oth_rows, 0:CUT]
        pending.append(send(piece, piece, wx_s.at[1, j - 1], wx_r.at[1, j - 1], dev_x(j)))
    landed(w_part.at[x, z, 1 - yh], wy_s.at[1], wy_r.at[1], dev_yh)
    send_v(1)
    send_states(0)
    run(fill_mix, 3, 4)
    local[2].wait()
    for n, yh_ in enumerate((yh, 1 - yh)):
        for j in (1, 2, 3):
            piece = w_all.at[w_rows(z, yh_, x_at(-j)), 0:CUT]
            landed(piece, wx_s.at[n, j - 1], wx_r.at[n, j - 1], dev_x(-j))
    send_p(0)
    send_z(0, 0)
    for d, sign in SIGNS:
        send_og(0, d, sign)
    pending.append(send(og_ref, og_rows(head), oc_s.at[0], oc_r.at[0], dev_core))

    run(fill_csel, 0, RESPS - 1)
    run(fill_mix, 5, 6)
    land_p(0)
    send_p(1)
    send_z(0, 1)
    run(fill_mix, 7)
    landed(states.at[slot_of(1 - yh, 0)], sy_s, sy_r, dev_yh)
    send_states(1)
    land_p(1)
    send_p(2)
    land_z(0, 0)
    send_z(1, 0)
    land_og(0)
    local[3].wait()
    land_v(0)
    land_v(1)
    for d, sign in SIGNS:
        piece = w_part.at[x]
        pending.append(send(piece, piece, vx_s.at[d], vx_r.at[d], dev_x(sign)))
    local[6].wait()
    run(forward_within, 0, 3)
    land_z(0, 1)
    send_z(1, 1)
    pass_states(0)
    land_og(1)
    land_p(2)
    send_p(3)
    land_z(1, 0)
    send_z(2, 0)
    run(forward_within, 4, 7)
    pass_states(1)
    land_z(1, 1)
    send_z(2, 1)
    for d, sign in SIGNS:
        landed(w_part.at[x_at(-sign)], vx_s.at[d], vx_r.at[d], dev_x(-sign))
        piece = part_half(-sign, d)
        pending.append(send(piece, piece, vf_s.at[d], vf_r.at[d], dev_x(sign)))
    local[5].wait()
    land_states(0)
    run(forward_own, 0, PAIRS - 1)
    land_og(2)
    land_p(3)
    land_z(2, 0)
    send_z(3, 0)
    land_states(1)
    run(forward_other, 0, PAIRS - 1)
    land_z(2, 1)
    send_z(3, 1)
    for d, sign in SIGNS:
        landed(part_half(2, d), vf_s.at[d], vf_r.at[d], dev_x(-sign))
    run(unpack, 0, NZ - 1)
    run(project, 3)
    run(project, 0)
    local[4].wait()
    landed(og_rows(yl * NCORE + 1 - core), oc_s.at[0], oc_r.at[0], dev_core)
    for d, sign in SIGNS:
        for i in range(3):

            @pl.when(has(-sign * (i + 1)))
            def _():
                piece = og_rows((yl - sign * (i + 1)) * NCORE + 1 - core)
                landed(piece, oc_s.at[1 + 3 * d + i], oc_r.at[1 + 3 * d + i], dev_core)

    run(backward, 0)
    share(3, 0)
    chain(3, near)
    share(0, 0)
    run(backward, 1)
    chain(0, near)
    chain(3, 1 - near)
    land_z(3, 0)
    land_z(3, 1)
    run(project, 1, 2)
    run(backward, 2)
    share(1, 0)
    chain(1, near)
    chain(0, 1 - near)
    run(add_x, 0)
    run(backward, 3)
    share(2, 0)
    chain(2, near)
    chain(1, 1 - near)
    run(add_x, 1)
    chain(2, 1 - near)
    run(add_x, 2)
    run(input_grad, 0, PAIRS - 1)
    run(add_x, 3)
    run(finish_layer, 0, NBLK - 1)
    run(finish_state, 0, NZ // 2 - 1)

    for copy in pending:
        copy.wait_send()
    for d, sign in SIGNS:
        for i in range(3):
            drain_og(i, d, sign)

            @pl.when(has(-sign * (i + 1)))
            def _():
                piece = og_rows((yl - sign * (i + 1)) * NCORE + core)
                sent(piece, piece, oc_s.at[1 + 3 * d + i], oc_r.at[1 + 3 * d + i], dev_core)

    def drain_g(u, carry):
        for j in (1, 2, 3):
            sent(
                g_piece(g_send, j, u), g_piece(g_recv, j, u),
                gx_s.at[j - 1, u], gx_r.at[j - 1, u], dev_x(j),
            )
        two = pl.ds(2 * u, 2)
        sent(gy_send.at[two], gy_recv.at[two], gy_s.at[u], gy_r.at[u], dev_yh)
        return carry

    run(drain_g, 0, NZ // 2 - 1)

    def drain_p(n, carry):
        sent(p_send.at[n], p_recv.at[n], pp_s.at[n], pp_r.at[n], dev_core)
        for d, sign in SIGNS:
            for o in (1, 2, 3):

                @pl.when(has(sign * o))
                def _():
                    sent(
                        r_send.at[d, o - 1, n], r_recv.at[d, o - 1, n],
                        rr_s.at[d, o - 1, n], rr_r.at[d, o - 1, n], dev_yl(sign),
                    )

        return carry

    run(drain_p, 0, NBLK - 1)


def copy_out(a, b, c, a_out, b_out, c_out):
    a_out[...] = a[...]
    b_out[...] = b[...]
    c_out[...] = c[...]


def per_device(
    ssm_input,
    b_proj,
    c_proj,
    step_size,
    a_log,
    d_skip,
    out_weight,
    prompt_state,
    prompt_of,
    out_grad,
):
    vmem = pl.BlockSpec(memory_space=pltpu.VMEM)
    anywhere = pl.BlockSpec(memory_space=pl.ANY)
    dma = pltpu.SemaphoreType.DMA
    sems = [
        (2,),
        (2, 3),
        (2, 4, 2),
        (2, 4),
        (2, NZ - 1),
        (2,),
        (2,),
        (),
        (2, 2),
        (2, 2),
        (2, 3),
        (7,),
        (3, NZ // 2),
        (NZ // 2,),
        (NBLK,),
        (2, 3, NBLK),
    ]
    sem_scratch = []
    for shape in sems:
        sem_scratch += [dma(shape), dma(shape)]
    shapes = (
        jax.ShapeDtypeStruct((RESP_ROWS, DW), BF16),
        jax.ShapeDtypeStruct((ROWS, WIDTH), BF16),
        jax.ShapeDtypeStruct((WIDTH, NS), F32),
    )
    results = pl.pallas_call(
        kernel,
        out_shape=shapes,
        in_specs=[pl.BlockSpec(memory_space=pltpu.SMEM)] + [vmem] * 3 + [anywhere] * 6,
        out_specs=(vmem, vmem, vmem),
        scratch_shapes=[
            pltpu.VMEM((ROWS, WIDTH), BF16),
            pltpu.VMEM((ROWS, NS), BF16),
            pltpu.VMEM((ROWS, NS), BF16),
            pltpu.VMEM((ROWS, HEADS), F32),
            pltpu.VMEM((WIDTH, DW), BF16),
            pltpu.VMEM((NX, NZ, NYH, SHARD, DW - CUT), BF16),
            pltpu.VMEM((ROWS, DW), BF16),
            pltpu.VMEM((GROUP, WIDTH, NS), BF16),
            pltpu.VMEM((ROWS, GROUP * NS), BF16),
            pltpu.VMEM((ROWS, WIDTH), F32),
            pltpu.VMEM((ROWS, WIDTH), BF16),
            pltpu.VMEM((ROWS, WIDTH), BF16),
            pltpu.VMEM((ROWS, WIDTH), F32),
            pltpu.VMEM((ROWS, WIDTH), BF16),
            pltpu.VMEM((ROWS, WIDTH), BF16),
            pltpu.VMEM((ROWS, BLK), F32),
            pltpu.VMEM((NBLK, NYL, RESP_ROWS, BLK), BF16),
            pltpu.VMEM((NBLK, NYL, RESP_ROWS, BLK), BF16),
            pltpu.VMEM((NBLK, NYL, RESP_ROWS, BLK), F32),
            pltpu.VMEM((2, 3, NBLK, RESP_ROWS, BLK), BF16),
            pltpu.VMEM((2, 3, NBLK, RESP_ROWS, BLK), BF16),
            pltpu.VMEM((2 * LANE, GROUP * NS), F32),
            pltpu.VMEM((NZ, NYH, LANE, NS), F32),
            pltpu.VMEM((3, NZ, NYH, LANE, NS), BF16),
            pltpu.VMEM((3, NZ, NYH, LANE, NS), BF16),
            pltpu.VMEM((NZ, LANE, NS), BF16),
            pltpu.VMEM((NZ, LANE, NS), BF16),
            dma((7,)),
        ]
        + sem_scratch,
        compiler_params=pltpu.CompilerParams(
            collective_id=0, has_side_effects=True, vmem_limit_bytes=56 * 1024 * 1024
        ),
        name="ssd_span",
    )(
        prompt_of,
        step_size.T,
        a_log.reshape(1, HEADS),
        d_skip.reshape(1, HEADS),
        ssm_input,
        b_proj,
        c_proj,
        out_weight,
        prompt_state.reshape(WIDTH, NS),
        out_grad,
    )
    parts = 4
    blocks = [
        pl.BlockSpec((shape.shape[0] // parts, shape.shape[1]), lambda i: (i, 0))
        for shape in shapes
    ]
    layer_out, grad_input, grad_state = pl.pallas_call(
        copy_out,
        grid=(parts,),
        out_shape=shapes,
        in_specs=blocks,
        out_specs=blocks,
        name="hand_out",
    )(*results)
    return layer_out, grad_input, grad_state.reshape(1, HEADS, WIDTH // HEADS, NS)


def solution(mesh):
    placed = (
        P("resp", "head"),
        P("resp", "head"),
        P("resp", "head"),
        P("resp", "head"),
        P("head"),
        P("head"),
        P(("head", "resp"), None),
        P("resp", "head", None, None),
        P("resp"),
        P(("resp", "head"), None),
    )
    return jax.shard_map(
        per_device,
        mesh=mesh,
        in_specs=placed,
        out_specs=(P(("resp", "head"), None), P("resp", "head"), P("resp", "head", None, None)),
        check_vma=False,
    )
```

time: 117 us -> 100 us (0.85)
  the two profiles are of different devices: /device:TPU:8 before, /device:TPU:16 now
where the time goes in v2:
time: 100 us
  Pallas kernels  99.4 us (99%)
    pallas_call x1, Pallas kernels, per_device(): pl.pallas_call(kernel, out_shape=shapes, in_specs=[pl.BlockSpec(memory_sp...  95.8 us
    pallas_call x1, Pallas kernels, per_device(): pl.pallas_call(copy_out, grid=(parts,), out_shape=shapes, in_specs=blocks...  3.65 us

profile of v2, /device:TPU:16, one launch (start us, length us, event | category | flops | bytes accessed | tf_op | source)
XLA Modules:
  0.0 100.0 jit_solution(9506262408018654766)
XLA Ops:
  0.6 95.8 %ssd_span.1 = (bf16[64,2048]{1,0:T(8,128)(2,1)}, bf16[512,1024]{1,0:T(8,128)(2,1)}, f32[1024,128]{1,0:T(8,128)}) custom-call(s32[8]{0:T(128)} %prompt_ref.1, f32[16,512]{1,0:T(8,128)} %bitcast.6, f32[1,16]{1,0:T(1,128)} %bitcast.7, f32[1,16]{1,0:T(1,128)} %bitcast.8, bf16[512,1024]{1,0:T(8,128)(2,1)} %x_hbm.1, bf16[512,128]{1,0:T(8,128)(2,1)} %b_hbm.1, ...), custom_call_target="tpu_custom_call" | custom-call | tf_op jit(solution)/shard_map/ssd_span/pallas_call | solution.py:763
  96.4 3.6 %hand_out.1 = (bf16[64,2048]{1,0:T(8,128)(2,1)}, bf16[512,1024]{1,0:T(8,128)(2,1)}, f32[1024,128]{1,0:T(8,128)}) custom-call(bf16[64,2048]{1,0:T(8,128)(2,1)} %get-tuple-element.9.a, bf16[512,1024]{1,0:T(8,128)(2,1)} %get-tuple-element.10.b, f32[1024,128]{1,0:T(8,128)} %get-tuple-element.11.c), custom_call_target="tpu_custom_call" | custom-call | tf_op jit(solution)/shard_map/hand_out/pallas_call | solution.py:820

commit v3 on v2

--- a/solution.py
+++ b/solution.py
@@ -24,6 +24,7 @@
 SHARD = 16
 LANE = 128
 PAIRS = WIDTH // LANE
+PARTS = 2
 NBLK = 4
 BLK = DW // NBLK
 EARLY = BLK
@@ -403,7 +404,7 @@
         return carry
 
     def carried(i, yh_):
-        cols = pl.ds(pl.multiple_of(i * LANE, LANE), LANE)
+        cols = pl.ds(pl.multiple_of(i * (2 * LANE), 2 * LANE), 2 * LANE)
         init = jnp.concatenate([states[yh_ * NX + k, cols, :] for k in range(NX)], axis=1)
         mine = csel[:, pl.ds(pl.multiple_of(yh_ * (NX * NS), NX * NS), NX * NS)]
         return cols, dot_nt(mine, init) * growth[:, cols]
@@ -571,6 +572,9 @@
     landed(w_part.at[x, z, 1 - yh], wy_s.at[1], wy_r.at[1], dev_yh)
     send_v(1)
     send_states(0)
+    for d, sign in SIGNS:
+        send_og(0, d, sign)
+    pending.append(send(og_ref, og_rows(head), oc_s.at[0], oc_r.at[0], dev_core))
     run(fill_mix, 3, 4)
     local[2].wait()
     for n, yh_ in enumerate((yh, 1 - yh)):
@@ -579,9 +583,6 @@
             landed(piece, wx_s.at[n, j - 1], wx_r.at[n, j - 1], dev_x(-j))
     send_p(0)
     send_z(0, 0)
-    for d, sign in SIGNS:
-        send_og(0, d, sign)
-    pending.append(send(og_ref, og_rows(head), oc_s.at[0], oc_r.at[0], dev_core))
 
     run(fill_csel, 0, RESPS - 1)
     run(fill_mix, 5, 6)
@@ -589,13 +590,13 @@
     send_p(1)
     send_z(0, 1)
     run(fill_mix, 7)
+    land_og(0)
     landed(states.at[slot_of(1 - yh, 0)], sy_s, sy_r, dev_yh)
     send_states(1)
     land_p(1)
     send_p(2)
     land_z(0, 0)
     send_z(1, 0)
-    land_og(0)
     local[3].wait()
     land_v(0)
     land_v(1)
@@ -622,13 +623,13 @@
         pending.append(send(piece, piece, vf_s.at[d], vf_r.at[d], dev_x(sign)))
     local[5].wait()
     land_states(0)
-    run(forward_own, 0, PAIRS - 1)
+    run(forward_own, 0, PAIRS // 2 - 1)
     land_og(2)
     land_p(3)
     land_z(2, 0)
     send_z(3, 0)
     land_states(1)
-    run(forward_other, 0, PAIRS - 1)
+    run(forward_other, 0, PAIRS // 2 - 1)
     land_z(2, 1)
     send_z(3, 1)
     for d, sign in SIGNS:
@@ -713,10 +714,22 @@
     run(drain_p, 0, NBLK - 1)
 
 
-def copy_out(a, b, c, a_out, b_out, c_out):
-    a_out[...] = a[...]
-    b_out[...] = b[...]
-    c_out[...] = c[...]
+def copy_out(*refs):
+    ins, outs, held, sems = refs[:3], refs[3:6], refs[6:9], refs[9]
+    into, out = [], []
+    for i, (a, b, v) in enumerate(zip(ins, outs, held)):
+        rows = a.shape[0] // PARTS
+        for p in range(PARTS):
+            piece = pl.ds(p * rows, rows)
+            into.append(pltpu.make_async_copy(a.at[piece], v.at[piece], sems.at[0, i, p]))
+            out.append(pltpu.make_async_copy(v.at[piece], b.at[piece], sems.at[1, i, p]))
+    for copy in into:
+        copy.start()
+    for first, second in zip(into, out):
+        first.wait()
+        second.start()
+    for copy in out:
+        copy.wait()
 
 
 def per_device(
@@ -812,17 +825,14 @@
         prompt_state.reshape(WIDTH, NS),
         out_grad,
     )
-    parts = 4
-    blocks = [
-        pl.BlockSpec((shape.shape[0] // parts, shape.shape[1]), lambda i: (i, 0))
-        for shape in shapes
-    ]
     layer_out, grad_input, grad_state = pl.pallas_call(
         copy_out,
-        grid=(parts,),
         out_shape=shapes,
-        in_specs=blocks,
-        out_specs=blocks,
+        in_specs=[anywhere] * 3,
+        out_specs=(anywhere,) * 3,
+        scratch_shapes=[pltpu.VMEM(shape.shape, shape.dtype) for shape in shapes]
+        + [dma((2, 3, PARTS))],
+        compiler_params=pltpu.CompilerParams(vmem_limit_bytes=56 * 1024 * 1024),
         name="hand_out",
     )(*results)
     return layer_out, grad_input, grad_state.reshape(1, HEADS, WIDTH // HEADS, NS)

time: 100 us -> 99.1 us (level)
  the two profiles are of different devices: /device:TPU:16 before, /device:TPU:8 now
where the time goes in v3:
time: 99.1 us; the launch traced here: 98.9 us
  Pallas kernels  98.2 us (99%)
    pallas_call x1, Pallas kernels, per_device(): pl.pallas_call(kernel, out_shape=shapes, in_specs=[pl.BlockSpec(memory_sp...  95.8 us
    pallas_call x1, Pallas kernels, per_device(): pl.pallas_call(copy_out, out_shape=shapes, in_specs=[anywhere] * 3, out_s...  2.42 us

profile of v3, /device:TPU:8, one launch (start us, length us, event | category | flops | bytes accessed | tf_op | source)
XLA Modules:
  0.0 98.9 jit_solution(16059558339505695434)
XLA Ops:
  0.6 95.8 %ssd_span.1 = (bf16[64,2048]{1,0:T(8,128)(2,1)}, bf16[512,1024]{1,0:T(8,128)(2,1)}, f32[1024,128]{1,0:T(8,128)}) custom-call(s32[8]{0:T(128)} %prompt_ref.1, f32[16,512]{1,0:T(8,128)} %bitcast.6, f32[1,16]{1,0:T(1,128)} %bitcast.7, f32[1,16]{1,0:T(1,128)} %bitcast.8, bf16[512,1024]{1,0:T(8,128)(2,1)} %x_hbm.1, bf16[512,128]{1,0:T(8,128)(2,1)} %b_hbm.1, ...), custom_call_target="tpu_custom_call" | custom-call | tf_op jit(solution)/shard_map/ssd_span/pallas_call | solution.py:776
  96.5 2.4 %hand_out.1 = (bf16[64,2048]{1,0:T(8,128)(2,1)}, bf16[512,1024]{1,0:T(8,128)(2,1)}, f32[1024,128]{1,0:T(8,128)}) custom-call(bf16[64,2048]{1,0:T(8,128)(2,1)} %get-tuple-element.9.refs_0_, bf16[512,1024]{1,0:T(8,128)(2,1)} %get-tuple-element.10.refs_1_, f32[1024,128]{1,0:T(8,128)} %get-tuple-element.11.refs_2_), custom_call_target="tpu_custom_call" | custom-call | tf_op jit(solution)/shard_map/hand_out/pallas_call | solution.py:828

commit v4 on v3

--- a/solution.py
+++ b/solution.py
@@ -56,6 +56,9 @@
     w_ref,
     state_ref,
     og_ref,
+    layer_hbm,
+    gin_hbm,
+    gstate_hbm,
     layer_ref,
     gin_ref,
     gstate_ref,
@@ -669,10 +672,18 @@
     run(add_x, 1)
     chain(2, 1 - near)
     run(add_x, 2)
+    results = [
+        pltpu.make_async_copy(gin_ref, gin_hbm, loc_sem.at[7]),
+        pltpu.make_async_copy(layer_ref, layer_hbm, loc_sem.at[8]),
+        pltpu.make_async_copy(gstate_ref, gstate_hbm, loc_sem.at[9]),
+    ]
     run(input_grad, 0, PAIRS - 1)
+    results[0].start()
     run(add_x, 3)
     run(finish_layer, 0, NBLK - 1)
+    results[1].start()
     run(finish_state, 0, NZ // 2 - 1)
+    results[2].start()
 
     for copy in pending:
         copy.wait_send()
@@ -712,6 +723,8 @@
         return carry
 
     run(drain_p, 0, NBLK - 1)
+    for copy in results:
+        copy.wait()
 
 
 def copy_out(*refs):
@@ -777,8 +790,11 @@
         kernel,
         out_shape=shapes,
         in_specs=[pl.BlockSpec(memory_space=pltpu.SMEM)] + [vmem] * 3 + [anywhere] * 6,
-        out_specs=(vmem, vmem, vmem),
+        out_specs=(anywhere,) * 3,
         scratch_shapes=[
+            pltpu.VMEM((RESP_ROWS, DW), BF16),
+            pltpu.VMEM((ROWS, WIDTH), BF16),
+            pltpu.VMEM((WIDTH, NS), F32),
             pltpu.VMEM((ROWS, WIDTH), BF16),
             pltpu.VMEM((ROWS, NS), BF16),
             pltpu.VMEM((ROWS, NS), BF16),
@@ -806,7 +822,7 @@
             pltpu.VMEM((3, NZ, NYH, LANE, NS), BF16),
             pltpu.VMEM((NZ, LANE, NS), BF16),
             pltpu.VMEM((NZ, LANE, NS), BF16),
-            dma((7,)),
+            dma((10,)),
         ]
         + sem_scratch,
         compiler_params=pltpu.CompilerParams(

time: 99.1 us -> 98.4 us (level)
  no operation moved by 1% of the time
where the time goes in v4:
time: 98.4 us; the launch traced here: 98.2 us
  Pallas kernels  97.6 us (99%)
    pallas_call x1, Pallas kernels, per_device(): pl.pallas_call(kernel, out_shape=shapes, in_specs=[pl.BlockSpec(memory_sp...  95.2 us
    pallas_call x1, Pallas kernels, per_device(): pl.pallas_call(copy_out, out_shape=shapes, in_specs=[anywhere] * 3, out_s...  2.42 us

profile of v4, /device:TPU:8, one launch (start us, length us, event | category | flops | bytes accessed | tf_op | source)
XLA Modules:
  0.0 98.2 jit_solution(12650656702288890835)
XLA Ops:
  0.6 95.2 %ssd_span.1 = (bf16[64,2048]{1,0:T(8,128)(2,1)}, bf16[512,1024]{1,0:T(8,128)(2,1)}, f32[1024,128]{1,0:T(8,128)}) custom-call(s32[8]{0:T(128)} %prompt_ref.1, f32[16,512]{1,0:T(8,128)} %bitcast.6, f32[1,16]{1,0:T(1,128)} %bitcast.7, f32[1,16]{1,0:T(1,128)} %bitcast.8, bf16[512,1024]{1,0:T(8,128)(2,1)} %x_hbm.1, bf16[512,128]{1,0:T(8,128)(2,1)} %b_hbm.1, ...), custom_call_target="tpu_custom_call" | custom-call | tf_op jit(solution)/shard_map/ssd_span/pallas_call | solution.py:789
  95.8 2.4 %hand_out.1 = (bf16[64,2048]{1,0:T(8,128)(2,1)}, bf16[512,1024]{1,0:T(8,128)(2,1)}, f32[1024,128]{1,0:T(8,128)}) custom-call(bf16[64,2048]{1,0:T(8,128)(2,1)} %get-tuple-element.9.refs_0_, bf16[512,1024]{1,0:T(8,128)(2,1)} %get-tuple-element.10.refs_1_, f32[1024,128]{1,0:T(8,128)} %get-tuple-element.11.refs_2_), custom_call_target="tpu_custom_call" | custom-call | tf_op jit(solution)/shard_map/hand_out/pallas_call | solution.py:844
